TPU v7x, 256 devices: a whole 4x4x8 slice. The times are simulated.
256 devices in a mesh: row: 16 (over y_hi, x, core), col: 16 (over z, y_lo).
Axes of the slice: x: 4, y: 4 (y_hi: 2, y_lo: 2; y = y_hi * 2 + y_lo), z: 8, core: 2. Of those that a mesh axis runs over, the one named last changes fastest.
Arguments:
- inputs: bfloat16 [1024, 8192], P('col', 'row'), may hold values from -6 to 6
- gate_weight: bfloat16 [8192, 12288], P('row', 'col'), may hold values from -0.0625 to 0.0625
- up_weight: bfloat16 [8192, 12288], P('row', 'col'), may hold values from -0.0625 to 0.0625
- down_weight: bfloat16 [12288, 8192], P('col', 'row'), may hold values from -0.0546875 to 0.0546875
- out_grad: bfloat16 [1024, 8192], P('col', 'row'), may hold values from -6 to 6
Outputs:
- output: bfloat16 [1024, 8192], P('col', 'row')
- input_grad: bfloat16 [1024, 8192], P('col', 'row')
- gate_grad: bfloat16 [8192, 12288], P('row', 'col')
- up_grad: bfloat16 [8192, 12288], P('row', 'col')
- down_grad: bfloat16 [12288, 8192], P('col', 'row')
All inputs are finite; a program needn't handle non-finite values.
Results may differ from a plain program's by a relative error of at most 0.005.
Values may be sent and summed in bfloat16 or wider, within the bound.
A program may use at most 64 MiB of HBM per device.

v0:
```python
import jax
import jax.numpy as jnp
from jax import lax
from jax.sharding import PartitionSpec as P


def contract_last(left, right):
    return lax.dot_general(
        left, right, (((1,), (1,)), ((), ())), preferred_element_type=jnp.float32
    )


def contract_first(left, right):
    return lax.dot_general(
        left, right, (((0,), (0,)), ((), ())), preferred_element_type=jnp.float32
    )


def body(inputs, gate_weight, up_weight, down_weight, out_grad):
    inputs_all = lax.all_gather(inputs, "col", axis=0, tiled=True)
    width = gate_weight.shape[1]
    rows = inputs_all
    gate_part = jnp.dot(rows, gate_weight, preferred_element_type=jnp.float32)
    up_part = jnp.dot(rows, up_weight, preferred_element_type=jnp.float32)
    joined = lax.psum_scatter(
        jnp.concatenate([gate_part, up_part], axis=1), "row", scatter_dimension=0, tiled=True
    )
    gate = joined[:, :width]
    up = joined[:, width:]
    sig = jax.nn.sigmoid(gate)
    act = gate * sig
    hidden = (act * up).astype(jnp.bfloat16)
    hidden_all = lax.all_gather(hidden, "row", axis=0, tiled=True)
    rows = hidden_all
    output = lax.psum_scatter(
        jnp.dot(rows, down_weight, preferred_element_type=jnp.float32),
        "col",
        scatter_dimension=0,
        tiled=True,
    ).astype(jnp.bfloat16)
    grads_all = lax.all_gather(out_grad, "col", axis=0, tiled=True)
    down_grad = contract_first(hidden_all, grads_all).astype(jnp.bfloat16)
    rows = grads_all
    hidden_grad = lax.psum_scatter(
        contract_last(rows, down_weight), "row", scatter_dimension=0, tiled=True
    )
    up_delta = (hidden_grad * act).astype(jnp.bfloat16)
    gate_delta = (hidden_grad * up * sig * (1.0 + gate * (1.0 - sig))).astype(jnp.bfloat16)
    gate_all, up_all = (
        lax.all_gather(gate_delta, "row", axis=0, tiled=True),
        lax.all_gather(up_delta, "row", axis=0, tiled=True),
    )
    input_grad = lax.psum_scatter(
        contract_last(gate_all, gate_weight) + contract_last(up_all, up_weight),
        "col",
        scatter_dimension=0,
        tiled=True,
    ).astype(jnp.bfloat16)
    gate_grad = contract_first(inputs_all, gate_all).astype(jnp.bfloat16)
    up_grad = contract_first(inputs_all, up_all).astype(jnp.bfloat16)
    return (output, input_grad, gate_grad, up_grad, down_grad)


def solution(mesh):
    return jax.shard_map(
        body,
        mesh=mesh,
        in_specs=(
            P("col", "row"),
            P("row", "col"),
            P("row", "col"),
            P("col", "row"),
            P("col", "row"),
        ),
        out_specs=(
            P("col", "row"),
            P("col", "row"),
            P("row", "col"),
            P("row", "col"),
            P("col", "row"),
        ),
        check_vma=False,
    )
```

profile of v0, /device:TPU:1, one launch (start us, length us, event | category | flops | bytes accessed | tf_op | source)
XLA Modules:
  0.0 653.1 jit_solution(3409588062728176174)
XLA Ops:
  7.2 0.0 copy-start
  7.2 0.0 all-gather.10.cloned.1.call-start
  7.2 0.7 all-gather.10.cloned.1.call-update
  7.9 0.0 all-gather.6.cloned.1.call-start
  8.0 0.7 all-gather.6.cloned.1.call-update
  8.7 0.0 reduce-scatter.15.cloned.1.call-start
  8.7 63.5 %all-gather.10.cloned.1.call-done = bf16[1024,512]{1,0:T(8,128)(2,1)} async-done(((bf16[64,512]{1,0:T(8,128)(2,1)}), bf16[1024,512]{1,0:T(8,128)(2,1)}) %all-gather.10.cloned.1.call-update) | async-done | bytes 1048592 | tf_op jit(solution)/shard_map/all_gather | solution.py:41
  72.2 4.1 fusion.6
  76.3 0.0 reduce-scatter.15.cloned.1.call-update
  76.3 0.0 copy-start.2
  76.3 0.0 reduce-scatter.13.cloned.1.call-start
  76.4 67.1 %all-gather.6.cloned.1.call-done = bf16[1024,512]{1,0:T(8,128)(2,1)} async-done(((bf16[64,512]{1,0:T(8,128)(2,1)}), bf16[1024,512]{1,0:T(8,128)(2,1)}) %all-gather.6.cloned.1.call-update) | async-done | bytes 1048592 | tf_op jit(solution)/shard_map/all_gather | solution.py:20
  143.5 0.0 copy-done
  143.5 0.0 copy-start.1
  143.5 2.3 fusion.3
  145.8 0.0 copy-done.2
  145.8 0.0 copy-done.1
  145.8 1.0 fusion.4
  146.9 3.2 pad_maximum_fusion
  150.0 6.6 %copy.27 = f32[1024,1536]{1,0:T(8,128)} copy(f32[1024,1536]{0,1:T(8,128)} %pad_maximum_fusion) | data formatting | bytes 12582912
  156.6 0.0 reduce-scatter.13.cloned.1.call-update
  156.6 0.0 all-gather.12.cloned.1.call-start
  156.7 83.8 %reduce-scatter.15.cloned.1.call-done = f32[64,768]{1,0:T(8,128)} async-done(((f32[1024,768]{1,0:T(8,128)}), f32[64,768]{1,0:T(8,128)}) %reduce-scatter.15.cloned.1.call-update) | async-done | bytes 196624 | tf_op jit(solution)/shard_map/reduce_scatter | solution.py:44
  240.5 100.4 %reduce-scatter.13.cloned.1.call-done = f32[64,1536]{1,0:T(8,128)} async-done(((f32[1024,1536]{1,0:T(8,128)}), f32[64,1536]{1,0:T(8,128)}) %reduce-scatter.13.cloned.1.call-update) | async-done | bytes 393232 | tf_op jit(solution)/shard_map/reduce_scatter | solution.py:25
  340.9 1.9 multiply_convert_fusion
  342.8 0.0 all-gather.12.cloned.1.call-update
  342.8 0.0 all-gather.14.cloned.1.call-start
  342.9 0.5 all-gather.14.cloned.1.call-update
  343.4 0.0 all-gather.8.cloned.1.call-start
  343.4 0.7 all-gather.8.cloned.1.call-update
  344.1 0.0 reduce-scatter.11.cloned.1.call-start
  344.2 52.2 %all-gather.12.cloned.1.call-done = bf16[1024,768]{1,0:T(8,128)(2,1)} async-done(((bf16[64,768]{1,0:T(8,128)(2,1)}), bf16[1024,768]{1,0:T(8,128)(2,1)}) %all-gather.12.cloned.1.call-update) | async-done | bytes 1572880 | tf_op jit(solution)/shard_map/all_gather | solution.py:50
  396.4 3.7 fusion.7
  400.1 50.1 %all-gather.14.cloned.1.call-done = bf16[1024,768]{1,0:T(8,128)(2,1)} async-done(((bf16[64,768]{1,0:T(8,128)(2,1)}), bf16[1024,768]{1,0:T(8,128)(2,1)}) %all-gather.14.cloned.1.call-update) | async-done | bytes 1572880 | tf_op jit(solution)/shard_map/all_gather | solution.py:51
  450.2 4.4 convolution_add_fusion
  454.6 0.0 copy-start.5
  454.6 0.0 reduce-scatter.11.cloned.1.call-update
  454.6 0.0 reduce-scatter.9.cloned.1.call-start
  454.7 49.5 %all-gather.8.cloned.1.call-done = bf16[1024,768]{1,0:T(8,128)(2,1)} async-done(((bf16[64,768]{1,0:T(8,128)(2,1)}), bf16[1024,768]{1,0:T(8,128)(2,1)}) %all-gather.8.cloned.1.call-update) | async-done | bytes 1572880 | tf_op jit(solution)/shard_map/all_gather | solution.py:33
  504.2 0.0 copy-done.5
  504.2 3.7 fusion.5
  508.0 0.0 copy-start.6
  508.0 0.0 reduce-scatter.9.cloned.1.call-update
  508.0 1.4 copy-done.6
  509.4 1.9 fusion
  511.3 0.0 copy-start.3
  511.3 2.4 copy.24
  513.7 0.0 copy-done.3
  513.7 1.9 fusion.1
  515.5 0.0 copy-start.4
  515.5 2.4 copy.25
  517.9 0.0 copy-done.4
  517.9 3.3 convolution_convert_fusion
  521.2 47.4 %reduce-scatter.11.cloned.1.call-done = f32[64,512]{1,0:T(8,128)} async-done(((f32[1024,512]{1,0:T(8,128)}), f32[64,512]{1,0:T(8,128)}) %reduce-scatter.11.cloned.1.call-update) | async-done | bytes 131088 | tf_op jit(solution)/shard_map/reduce_scatter | solution.py:53
  568.6 1.5 convert_element_type.34
  570.2 74.8 %reduce-scatter.9.cloned.1.call-done = f32[64,512]{1,0:T(8,128)} async-done(((f32[1024,512]{1,0:T(8,128)}), f32[64,512]{1,0:T(8,128)}) %reduce-scatter.9.cloned.1.call-update) | async-done | bytes 131088 | tf_op jit(solution)/shard_map/reduce_scatter | solution.py:35
  645.0 1.5 convert_element_type.31
Async XLA Ops:
  7.2 136.3 %copy-start = (bf16[512,768]{1,0:T(8,128)(2,1)S(1)}, bf16[512,768]{1,0:T(8,128)(2,1)}, u32[]{:S(2)}) copy-start(bf16[512,768]{1,0:T(8,128)(2,1)} %param.6) | copy-start | bytes 2359300
  7.2 65.0 %all-gather.10.cloned.1.call-start = ((), (), s32[]{:S(2)}) async-start(), calls=%async_computation.7 | async-start | bytes 1114112 | tf_op jit(solution)/shard_map/all_gather | solution.py:41
  7.9 135.5 %all-gather.6.cloned.1.call-start = ((), (), s32[]{:S(2)}) async-start(), calls=%async_computation.4 | async-start | bytes 1114112 | tf_op jit(solution)/shard_map/all_gather | solution.py:20
  8.7 231.8 %reduce-scatter.15.cloned.1.call-start = ((), (), s32[]{:S(2)}) async-start(), calls=%async_computation.12 | async-start | bytes 3342336 | tf_op jit(solution)/shard_map/reduce_scatter | solution.py:44
  76.3 69.5 %copy-start.2 = (bf16[512,768]{1,0:T(8,128)(2,1)S(1)}, bf16[512,768]{1,0:T(8,128)(2,1)}, u32[]{:S(2)}) copy-start(bf16[512,768]{1,0:T(8,128)(2,1)} %param.7) | copy-start | bytes 2359300
  76.3 264.5 %reduce-scatter.13.cloned.1.call-start = ((), (), s32[]{:S(2)}) async-start(), calls=%async_computation.11 | async-start | bytes 6684672 | tf_op jit(solution)/shard_map/reduce_scatter | solution.py:25
  143.5 2.4 copy-start.1
  156.6 239.8 %all-gather.12.cloned.1.call-start = ((), (), s32[]{:S(2)}) async-start(), calls=%async_computation.8 | async-start | bytes 1671168 | tf_op jit(solution)/shard_map/all_gather | solution.py:50
  342.8 107.4 %all-gather.14.cloned.1.call-start = ((), (), s32[]{:S(2)}) async-start(), calls=%async_computation.9 | async-start | bytes 1671168 | tf_op jit(solution)/shard_map/all_gather | solution.py:51
  343.4 160.9 %all-gather.8.cloned.1.call-start = ((), (), s32[]{:S(2)}) async-start(), calls=%async_computation.5 | async-start | bytes 1671168 | tf_op jit(solution)/shard_map/all_gather | solution.py:33
  344.1 224.5 %reduce-scatter.11.cloned.1.call-start = ((), (), s32[]{:S(2)}) async-start(), calls=%async_computation.10 | async-start | bytes 2228224 | tf_op jit(solution)/shard_map/reduce_scatter | solution.py:53
  454.6 49.6 %copy-start.5 = (bf16[768,512]{1,0:T(8,128)(2,1)S(1)}, bf16[768,512]{1,0:T(8,128)(2,1)}, u32[]{:S(2)}) copy-start(bf16[768,512]{1,0:T(8,128)(2,1)} %param.8) | copy-start | bytes 2359300
  454.6 190.3 %reduce-scatter.9.cloned.1.call-start = ((), (), s32[]{:S(2)}) async-start(), calls=%async_computation.6 | async-start | bytes 2228224 | tf_op jit(solution)/shard_map/reduce_scatter | solution.py:35
  508.0 1.4 copy-start.6
  511.3 2.4 copy-start.3
  515.5 2.4 copy-start.4
Sparse Core Ops, SparseCore 0:
  9.8 62.3 all-gather.9
  74.0 69.4 all-gather.5
  147.8 92.6 reduce-scatter.14
  244.8 96.0 reduce-scatter.12
  344.0 52.3 all-gather.11
  399.5 50.6 all-gather.13
  453.6 50.6 all-gather.7
  506.8 61.8 reduce-scatter.10
  571.2 73.7 reduce-scatter.8
where the time goes:
time: 664 us; the launch traced here: 653 us
  waiting for transfers between devices  592 us (89%)
  matrix products  26.3 us (4%)
  between operations  13.9 us (2%)
  local copies, waits for them, and re-layouts  12.8 us (2%)
  other arithmetic  8.18 us (1%)
    reduce_scatter x1, waiting for transfers between devices, body(): lax.psum_scatter(jnp.concatenate([gate_part, up_part], axis=1), 'row', sc...  100 us
    reduce_scatter x1, waiting for transfers between devices, body(): lax.psum_scatter(contract_last(rows, down_weight), 'row', scatter_dimensi...  83.8 us
    reduce_scatter x1, waiting for transfers between devices, body(): lax.psum_scatter(jnp.dot(rows, down_weight, preferred_element_type=jnp.fl...  74.8 us
    all_gather x1, waiting for transfers between devices, body(): inputs_all = lax.all_gather(inputs, 'col', axis=0, tiled=True)  67.1 us
    all_gather x1, waiting for transfers between devices, body(): grads_all = lax.all_gather(out_grad, 'col', axis=0, tiled=True)  63.5 us
    all_gather x1, waiting for transfers between devices, body(): lax.all_gather(gate_delta, 'row', axis=0, tiled=True)  52.2 us
    all_gather x1, waiting for transfers between devices, body(): lax.all_gather(up_delta, 'row', axis=0, tiled=True)  50.1 us
    all_gather x1, waiting for transfers between devices, body(): hidden_all = lax.all_gather(hidden, 'row', axis=0, tiled=True)  49.5 us
  transfers between devices with their start and end apart: 9, of which 9 were waited for; matrix products, arithmetic and copies ran while one was open for 6% of the time, Pallas kernels for 0%

commit v1 on v0

v1 whole, which is shorter than its diff:
```python
import jax
import jax.numpy as jnp
from jax import lax
from jax.experimental import pallas as pl
from jax.experimental.pallas import tpu as pltpu
from jax.sharding import PartitionSpec as P

MESH = pl.DeviceIdType.MESH
F32 = jnp.float32
BF16 = jnp.bfloat16
B = 64
F = 512
H = 768
T = 256
ORDER = (4, 3, 5, 2, 6, 1, 7, 0)


def nn(left, right):
    return jnp.dot(left, right, preferred_element_type=F32)


def nt(left, right):
    return lax.dot_general(left, right, (((1,), (1,)), ((), ())), preferred_element_type=F32)


def tn(left, right):
    return lax.dot_general(left, right, (((0,), (0,)), ((), ())), preferred_element_type=F32)


def tiles(count, body):
    def step(i, carry):
        body(pl.multiple_of(i * T, T))
        return carry

    lax.fori_loop(0, count, step, 0)


class Ring:
    def __init__(self, size, pos, neighbour, partner, view, send, recv, psend, precv, pending):
        self.size, self.pos, self.neighbour, self.partner, self.view = size, pos, neighbour, partner, view
        self.sems, self.psems, self.pending = (send, recv), (psend, precv), pending

    def at(self, dist, way):
        step = 1 if way == 0 else -1
        return lax.rem(self.pos - step * dist + self.size, self.size)

    def copy(self, lane, dist, way, origin):
        ref = self.view(lane, origin)
        if 2 * dist == self.size:
            ref = ref.at[pl.ds(way * (B // 2), B // 2)]
        return pltpu.make_async_remote_copy(
            src_ref=ref,
            dst_ref=ref,
            send_sem=self.sems[0].at[way, lane, dist - 1],
            recv_sem=self.sems[1].at[way, lane, dist - 1],
            device_id=self.neighbour(way),
            device_id_type=MESH,
        )

    def send(self, lane, dist, way):
        copy = self.copy(lane, dist, way, self.at(dist - 1, way))
        copy.start()
        self.pending.append(copy)

    def wait(self, lane, dist, way):
        self.copy(lane, dist, way, self.at(dist, way)).wait_recv()

    def pair_copy(self, lane):
        ref = self.view(lane, self.pos)
        return pltpu.make_async_remote_copy(
            src_ref=ref, dst_ref=ref, send_sem=self.psems[0], recv_sem=self.psems[1],
            device_id=self.partner, device_id_type=MESH,
        )

    def send_pair(self):
        copy = self.pair_copy(0)
        copy.start()
        self.pending.append(copy)

    def wait_pair(self):
        self.pair_copy(1).wait_recv()


def kernel(
    x_hbm, wg_hbm, wu_hbm, wd_hbm, g_hbm,
    out_ref, ing_ref, gg_ref, ug_ref, dg_ref,
    xall, gall, xsib, gsib, wg, wu, wd, wgs, wus, wds,
    pg, ph, rg, rh, og, oh, acc, hall, dall, gu,
    po, pof, ro, so, zo, pi, pif, ri, si, zi, own,
    lsem, wsend, wrecv,
    xs, xr, xps, xpr, gs, gr, gps, gpr,
    xss, xsr, gss, gsr,
    rgs, rgr, rhs, rhr,
    hs, hr, hps, hpr, ds, dr, dps, dpr,
    hss, hsr, dss, dsr,
    ys, yr, zs, zr,
):
    r = lax.axis_index("row")
    c = lax.axis_index("col")
    yh, x, k = r // 8, (r // 2) % 4, r % 2
    z, yl = c // 2, c % 2
    me = yh * 4 + x
    pending = []

    sibling = (yh * 8 + x * 2 + (1 - k), c)
    yl_partner = (r, z * 2 + (1 - yl))
    yh_partner = ((1 - yh) * 8 + x * 2 + k, c)

    def z_dev(d):
        return (r, lax.rem(z + d, 8) * 2 + yl)

    def x_dev(d):
        return (yh * 8 + lax.rem(x + d, 4) * 2 + k, c)

    def row_dev(d):
        return (lax.rem(yh + d // 4, 2) * 8 + lax.rem(x + d % 4, 4) * 2 + k, c)

    def remote(src, dst, send, recv, device):
        return pltpu.make_async_remote_copy(
            src_ref=src, dst_ref=dst, send_sem=send, recv_sem=recv, device_id=device, device_id_type=MESH
        )

    def push(src, dst, send, recv, device):
        copy = remote(src, dst, send, recv, device)
        copy.start()
        pending.append(copy)

    local = [
        pltpu.make_async_copy(src, dst, lsem.at[i])
        for i, (src, dst) in enumerate((
            (x_hbm, xall.at[yl, z]), (g_hbm, gall.at[yl, z]), (wg_hbm, wg), (wu_hbm, wu), (wd_hbm, wd),
        ))
    ]
    for copy in local:
        copy.start()
    barrier = pltpu.get_barrier_semaphore()
    peers = [sibling, yl_partner] + [z_dev(d) for d in range(1, 8)] + [row_dev(d) for d in range(1, 8)]
    for peer in peers:
        pl.semaphore_signal(barrier, inc=1, device_id=peer, device_id_type=MESH)
    pl.semaphore_wait(barrier, len(peers))

    def lane_yl(lane):
        return yl if lane == 0 else 1 - yl

    def z_next(way):
        return z_dev(1 if way == 0 else 7)

    def x_next(way):
        return x_dev(1 if way == 0 else 3)

    ring_x = Ring(8, z, z_next, yl_partner, lambda lane, p: xall.at[lane_yl(lane), p], xs, xr, xps, xpr, pending)
    ring_g = Ring(8, z, z_next, yl_partner, lambda lane, p: gall.at[lane_yl(lane), p], gs, gr, gps, gpr, pending)

    def to_sibling(full, half, send, recv, p, d):
        push(full.at[1 - k, p], half.at[p], send.at[d], recv.at[d], sibling)

    def ring_start(ring):
        ring.send_pair()
        for way in (0, 1):
            ring.send(0, 1, way)

    def ring_pair(ring, full, half, send, recv):
        ring.wait_pair()
        for way in (0, 1):
            ring.send(1, 1, way)
        to_sibling(full, half, send, recv, z, 0)

    def ring_step(ring, dist, full, half, send, recv):
        for lane in (0, 1):
            for way in (0, 1):
                ring.wait(lane, dist, way)
                if dist < 4:
                    ring.send(lane, dist + 1, way)
        if dist < 4:
            for way in (0, 1):
                to_sibling(full, half, send, recv, ring.at(dist, way), dist if way == 0 else 8 - dist)
        else:
            to_sibling(full, half, send, recv, ring.at(dist, 0), dist)

    xargs = (xall, xsib, xss, xsr)
    gargs = (gall, gsib, gss, gsr)
    local[0].wait()
    ring_start(ring_x)
    local[1].wait()
    ring_start(ring_g)
    for i, (src, dst) in enumerate(((wg, wgs), (wu, wus), (wd, wds))):
        local[2 + i].wait()
        push(src, dst, wsend.at[i], wrecv.at[i], sibling)
    ring_pair(ring_x, *xargs)
    ring_step(ring_x, 1, *xargs)
    ring_pair(ring_g, *gargs)
    ring_step(ring_x, 2, *xargs)
    ring_step(ring_g, 1, *gargs)
    ring_step(ring_x, 3, *xargs)
    ring_step(ring_g, 2, *gargs)
    ring_step(ring_x, 4, *xargs)

    def wait_sibling(half, send, recv):
        for d in range(8):
            p = lax.rem(z - d + 8, 8)
            remote(half.at[p], half.at[p], send.at[d], recv.at[d], sibling).wait_recv()

    wait_sibling(xsib, xss, xsr)
    for i, dst in enumerate((wgs, wus, wds)):
        remote(dst, dst, wsend.at[i], wrecv.at[i], sibling).wait_recv()

    def put_partial(value, part, part_own, col):
        acc[...] = value
        part[:, :, pl.ds(col, T)] = value.astype(BF16).reshape(8, B, T)
        part_own[:, pl.ds(col, T)] = acc[pl.ds(pl.multiple_of(me * B, B), B), :]

    for j, (w, ws) in enumerate(((wg, wgs), (wu, wus))):
        def gate_up(col, w=w, ws=ws, j=j):
            value = nn(xall[k].reshape(8 * B, F), w[:, pl.ds(col, T)])
            value += nn(xsib[...].reshape(8 * B, F), ws[:, pl.ds(col, T)])
            put_partial(value, pg, og, pl.multiple_of(j * H + col, T))

        tiles(H // T, gate_up)

    def row_target(d):
        return lax.rem(yh + d // 4, 2) * 4 + lax.rem(x + d % 4, 4)

    for d in range(1, 8):
        push(pg.at[row_target(d)], rg.at[d - 1], rgs.at[d - 1], rgr.at[d - 1], row_dev(d))

    ring_step(ring_g, 3, *gargs)
    ring_step(ring_g, 4, *gargs)
    wait_sibling(gsib, gss, gsr)

    def hidden_grad_tile(col):
        value = nt(gall[k].reshape(8 * B, F), wd[pl.ds(col, T), :])
        value += nt(gsib[...].reshape(8 * B, F), wds[pl.ds(col, T), :])
        put_partial(value, ph, oh, col)

    tiles(H // T, hidden_grad_tile)
    for d in range(1, 8):
        push(ph.at[row_target(d)], rh.at[d - 1], rhs.at[d - 1], rhr.at[d - 1], row_dev(d))

    for d in range(1, 8):
        remote(rg.at[d - 1], rg.at[d - 1], rgs.at[d - 1], rgr.at[d - 1], row_dev(d)).wait_recv()

    def hidden_tile(col):
        up_col = pl.multiple_of(H + col, T)
        gate, up = og[:, pl.ds(col, T)], og[:, pl.ds(up_col, T)]
        for d in range(7):
            gate += rg[d, :, pl.ds(col, T)].astype(F32)
            up += rg[d, :, pl.ds(up_col, T)].astype(F32)
        gu[:, pl.ds(col, T)] = gate
        gu[:, pl.ds(up_col, T)] = up
        hall[k, me, :, pl.ds(col, T)] = (gate * jax.nn.sigmoid(gate) * up).astype(BF16)

    tiles(H // T, hidden_tile)

    def lane_slot(lane, p):
        return (yh if lane == 0 else 1 - yh) * 4 + p

    ring_h = Ring(4, x, x_next, yh_partner, lambda lane, p: hall.at[k, lane_slot(lane, p)], hs, hr, hps, hpr, pending)
    ring_d = Ring(4, x, x_next, yh_partner, lambda lane, p: dall.at[k, lane_slot(lane, p)], ds, dr, dps, dpr, pending)

    def swap(full, send, recv, lane, p, i):
        ref = full.at[k, lane_slot(lane, p)]
        push(ref, ref, send.at[i], recv.at[i], sibling)

    def row_start(ring, full, send, recv):
        ring.send_pair()
        for way in (0, 1):
            ring.send(0, 1, way)
        swap(full, send, recv, 0, x, 0)

    def row_rest(ring, full, send, recv):
        ring.wait_pair()
        for way in (0, 1):
            ring.send(1, 1, way)
        swap(full, send, recv, 1, x, 4)
        for lane in (0, 1):
            for way in (0, 1):
                ring.wait(lane, 1, way)
                ring.send(lane, 2, way)
                swap(full, send, recv, lane, ring.at(1, way), lane * 4 + 1 + 2 * way)
        for lane in (0, 1):
            for way in (0, 1):
                ring.wait(lane, 2, way)
            swap(full, send, recv, lane, ring.at(2, 0), lane * 4 + 2)

    def row_swapped(full, send, recv):
        for lane in (0, 1):
            for d in range(4):
                i = lane * 4 + d
                ref = full.at[1 - k, lane_slot(lane, lax.rem(x - d + 4, 4))]
                remote(ref, ref, send.at[i], recv.at[i], sibling).wait_recv()

    hargs = (ring_h, hall, hss, hsr)
    dargs = (ring_d, dall, dss, dsr)
    row_start(*hargs)

    for d in range(1, 8):
        remote(rh.at[d - 1], rh.at[d - 1], rhs.at[d - 1], rhr.at[d - 1], row_dev(d)).wait_recv()

    def delta_tile(col):
        up_col = pl.multiple_of(H + col, T)
        hidden_grad = oh[:, pl.ds(col, T)]
        for d in range(7):
            hidden_grad += rh[d, :, pl.ds(col, T)].astype(F32)
        gate, up = gu[:, pl.ds(col, T)], gu[:, pl.ds(up_col, T)]
        sig = jax.nn.sigmoid(gate)
        dall[k, me, :, pl.ds(up_col, T)] = (hidden_grad * (gate * sig)).astype(BF16)
        dall[k, me, :, pl.ds(col, T)] = (hidden_grad * up * sig * (1.0 + gate * (1.0 - sig))).astype(BF16)

    tiles(H // T, delta_tile)
    row_start(*dargs)
    row_rest(*hargs)
    row_swapped(hall, hss, hsr)

    def start_pair(part, received, base):
        for d in ORDER:
            p = lax.rem(z + d, 8)
            push(part.at[p], received.at[p], ys.at[base, d], yr.at[base, d], yl_partner)

    def pair_step(part_own, received, summed, landed, base, d):
        p = lax.rem(z + d, 8)
        remote(received.at[p], received.at[p], ys.at[base, d], yr.at[base, d], yl_partner).wait_recv()
        total = part_own[p] + received[p].astype(F32)
        if d == 0:
            own[base] = total
        else:
            summed[p] = total.astype(BF16)
            push(summed.at[p], landed.at[d - 1], zs.at[base, d - 1], zr.at[base, d - 1], z_dev(d))

    def finish(landed, base, result):
        for d in range(1, 8):
            remote(landed.at[d - 1], landed.at[d - 1], zs.at[base, d - 1], zr.at[base, d - 1], z_dev(d)).wait_recv()
        total = own[base]
        for d in range(7):
            total += landed[d].astype(F32)
        result[...] = total.astype(BF16)

    def out_away(col):
        po[:, :, pl.ds(col, T)] = nn(hall[1 - yl].reshape(8 * B, H), wd[:, pl.ds(col, T)]).astype(BF16).reshape(8, B, T)

    def out_home(col):
        pof[:, :, pl.ds(col, T)] = nn(hall[yl].reshape(8 * B, H), wd[:, pl.ds(col, T)]).reshape(8, B, T)

    tiles(F // T, out_away)
    start_pair(po, ro, 0)
    tiles(F // T, out_home)
    row_rest(*dargs)

    for d in ORDER:
        pair_step(pof, ro, so, zo, 0, d)

    row_swapped(dall, dss, dsr)

    def ing_tile(half, col):
        left = dall[half].reshape(8 * B, 2 * H)
        return nt(left[:, :H], wg[pl.ds(col, T), :]) + nt(left[:, H:], wu[pl.ds(col, T), :])

    def ing_away(col):
        pi[:, :, pl.ds(col, T)] = ing_tile(1 - yl, col).astype(BF16).reshape(8, B, T)

    def ing_home(col):
        pif[:, :, pl.ds(col, T)] = ing_tile(yl, col).reshape(8, B, T)

    tiles(F // T, ing_away)
    start_pair(pi, ri, 1)
    tiles(F // T, ing_home)

    def gate_grad_tile(col):
        gg_ref[:, pl.ds(col, T)] = tn(xall[...].reshape(16 * B, F), dall[:, :, :, pl.ds(col, T)].reshape(16 * B, T)).astype(BF16)

    def up_grad_tile(col):
        up_col = pl.multiple_of(H + col, T)
        ug_ref[:, pl.ds(col, T)] = tn(xall[...].reshape(16 * B, F), dall[:, :, :, pl.ds(up_col, T)].reshape(16 * B, T)).astype(BF16)

    def down_grad_tile(col):
        dg_ref[pl.ds(col, T), :] = tn(hall[:, :, :, pl.ds(col, T)].reshape(16 * B, T), gall[...].reshape(16 * B, F)).astype(BF16)

    for i, d in enumerate(ORDER):
        pair_step(pif, ri, si, zi, 1, d)
        if i == 3:
            tiles(H // T, gate_grad_tile)
    tiles(H // T, up_grad_tile)
    tiles(H // T, down_grad_tile)
    finish(zo, 0, out_ref)
    finish(zi, 1, ing_ref)
    for copy in pending:
        copy.wait_send()


def body(inputs, gate_weight, up_weight, down_weight, out_grad):
    dma = pltpu.SemaphoreType.DMA
    bf = lambda *shape: pltpu.VMEM(shape, BF16)
    f32 = lambda *shape: pltpu.VMEM(shape, F32)
    ring8 = [dma((2, 2, 4)), dma((2, 2, 4)), dma, dma]
    ring4 = [dma((2, 2, 2)), dma((2, 2, 2)), dma, dma]
    return pl.pallas_call(
        kernel,
        out_shape=(
            jax.ShapeDtypeStruct((B, F), BF16),
            jax.ShapeDtypeStruct((B, F), BF16),
            jax.ShapeDtypeStruct((F, H), BF16),
            jax.ShapeDtypeStruct((F, H), BF16),
            jax.ShapeDtypeStruct((H, F), BF16),
        ),
        in_specs=[pl.BlockSpec(memory_space=pl.ANY)] * 5,
        out_specs=(pl.BlockSpec(memory_space=pltpu.VMEM),) * 5,
        scratch_shapes=[
            bf(2, 8, B, F), bf(2, 8, B, F), bf(8, B, F), bf(8, B, F),
            bf(F, H), bf(F, H), bf(H, F), bf(F, H), bf(F, H), bf(H, F),
            bf(8, B, 2 * H), bf(8, B, H), bf(7, B, 2 * H), bf(7, B, H),
            f32(B, 2 * H), f32(B, H), f32(8 * B, T),
            bf(2, 8, B, H), bf(2, 8, B, 2 * H), f32(B, 2 * H),
            bf(8, B, F), f32(8, B, F), bf(8, B, F), bf(8, B, F), bf(7, B, F),
            bf(8, B, F), f32(8, B, F), bf(8, B, F), bf(8, B, F), bf(7, B, F),
            f32(2, B, F),
            dma((5,)), dma((3,)), dma((3,)),
            *ring8, *ring8,
            dma((8,)), dma((8,)), dma((8,)), dma((8,)),
            dma((7,)), dma((7,)), dma((7,)), dma((7,)),
            *ring4, *ring4,
            dma((8,)), dma((8,)), dma((8,)), dma((8,)),
            dma((2, 8)), dma((2, 8)), dma((2, 7)), dma((2, 7)),
        ],
        compiler_params=pltpu.CompilerParams(collective_id=0, has_side_effects=True, vmem_limit_bytes=52 << 20),
        name="ffn",
    )(inputs, gate_weight, up_weight, down_weight, out_grad)


def solution(mesh):
    return jax.shard_map(
        body,
        mesh=mesh,
        in_specs=(P("col", "row"), P("row", "col"), P("row", "col"), P("col", "row"), P("col", "row")),
        out_specs=(P("col", "row"), P("col", "row"), P("row", "col"), P("row", "col"), P("col", "row")),
        check_vma=False,
    )
```

time: 664 us -> 130 us (0.20); the launches traced: 653 us -> 129 us
  waiting for transfers between devices: 592 us -> 0 us
  Pallas kernels: 0 us -> 123 us
  matrix products: 26.3 us -> 0 us
  between operations: 13.9 us -> 0.65 us
  other arithmetic: 8.18 us -> 0 us
  local copies, waits for them, and re-layouts: 12.8 us -> 6.11 us
    reduce_scatter x4 -> x0, waiting for transfers between devices: 306 us -> none  [the longest x1 100 us: body(): lax.psum_scatter(jnp.concatenate([gate_part, up_part], axis=1), 'row', sc...]
    all_gather x5 -> x0, waiting for transfers between devices: 282 us -> none  [the longest x1 67.1 us: body(): inputs_all = lax.all_gather(inputs, 'col', axis=0, tiled=True)]
    pallas_call x0 -> x1, Pallas kernels: none -> 123 us  [body(): pl.pallas_call(kernel, out_shape=(jax.ShapeDtypeStruct((B, F), BF16), jax...]
    dot_general x8 -> x0, matrix products: 22.2 us -> none  [the longest x2 8.09 us: contract_last(): lax.dot_general(left, right, (((1,), (1,)), ((), ())), preferred_element_...]
    unnamed x17 -> x11, local copies, waits for them, and re-layouts: 12.8 us -> 6.11 us
  transfers between devices with their start and end apart: 9 -> 0, of which waited for: 9 -> 0; matrix products, arithmetic and copies ran while one was open for 6% -> 0% of each run, Pallas kernels for 0% -> 0%
where the time goes in v1:
time: 130 us; the launch traced here: 129 us
  Pallas kernels  123 us (95%)
  local copies, waits for them, and re-layouts  6.11 us (5%)
    pallas_call x1, Pallas kernels, body(): pl.pallas_call(kernel, out_shape=(jax.ShapeDtypeStruct((B, F), BF16), jax...  123 us
    unnamed x11, local copies, waits for them, and re-layouts  6.11 us

profile of v1, /device:TPU:1, one launch (start us, length us, event | category | flops | bytes accessed | tf_op | source)
XLA Modules:
  0.0 129.4 jit_solution(17405336142006966934)
XLA Ops:
  0.6 0.0 copy-start
  0.6 0.8 copy-done
  1.5 0.0 copy-start.1
  1.5 0.8 copy-done.1
  2.3 122.6 %ffn.1 = (bf16[64,512]{1,0:T(8,128)(2,1)S(1)}, bf16[64,512]{1,0:T(8,128)(2,1)S(1)}, bf16[512,768]{1,0:T(8,128)(2,1)S(1)}, bf16[512,768]{1,0:T(8,128)(2,1)S(1)}, bf16[768,512]{1,0:T(8,128)(2,1)}) custom-call(bf16[64,512]{1,0:T(8,128)(2,1)S(1)} %copy-done, bf16[512,768]{1,0:T(8,128)(2,1)} %wg_hbm.1, bf16[512,768]{1,0:T(8,128)(2,1)} %wu_hbm.1, ...), custom_call_target="tpu_custom_call" | custom-call | tf_op jit(solution)/shard_map/ffn/pallas_call | solution.py:395
  125.0 0.6 copy.15
  125.6 0.6 copy.16
  126.2 0.9 copy.17
  127.1 0.0 copy-start.2
  127.1 0.9 copy.18
  128.0 0.5 copy-done.2
  128.5 0.9 copy.19
Async XLA Ops:
  0.6 0.8 copy-start
  1.5 0.8 copy-start.1
  127.1 1.4 %copy-start.2 = (bf16[768,512]{1,0:T(8,128)(2,1)S(1)}, bf16[768,512]{1,0:T(8,128)(2,1)}, u32[]{:S(2)}) copy-start(bf16[768,512]{1,0:T(8,128)(2,1)} %get-tuple-element.14) | copy-start | bytes 2359300

commit v2 on v0

v2 whole, which is shorter than its diff:
```python
import jax
import jax.numpy as jnp
from jax import lax
from jax.experimental import pallas as pl
from jax.experimental.pallas import tpu as pltpu
from jax.sharding import PartitionSpec as P

MESH = pl.DeviceIdType.MESH
F32 = jnp.float32
BF16 = jnp.bfloat16
B = 64
F = 512
H = 768
T = 256
NEAR = (0, 1, 7, 2, 6, 3, 5, 4)
SLOT = tuple(NEAR.index(d) for d in range(8))
FAR_A = (3, 1, 2, 0)
FAR_B = (7, 5, 6, 4)
C = 4 * B
R = 32


def nn(left, right):
    return jnp.dot(left, right, preferred_element_type=F32)


def nt(left, right):
    return lax.dot_general(left, right, (((1,), (1,)), ((), ())), preferred_element_type=F32)


def tn(left, right):
    return lax.dot_general(left, right, (((0,), (0,)), ((), ())), preferred_element_type=F32)


def tiles(count, body):
    def step(i, carry):
        body(pl.multiple_of(i * T, T))
        return carry

    lax.fori_loop(0, count, step, 0)


class Ring:
    def __init__(self, far, src, dst, view, half, neighbour, sems, pending):
        self.far, self.src, self.dst, self.view, self.half = far, src, dst, view, half
        self.neighbour, self.sems, self.pending = neighbour, sems, pending

    def copy(self, src, dst, lane, dist, way):
        if dist == self.far:
            src, dst = self.half(src, way), self.half(dst, way)
        sems = [sem.at[way, lane, dist - 1] for sem in self.sems]
        return pltpu.make_async_remote_copy(
            src_ref=src, dst_ref=dst, send_sem=sems[0], recv_sem=sems[1],
            device_id=self.neighbour(way), device_id_type=MESH,
        )

    def send(self, lane, dist, way):
        copy = self.copy(self.src(lane, dist - 1, way), self.dst(lane, dist, way), lane, dist, way)
        copy.start()
        self.pending.append(copy)

    def wait(self, lane, dist, way):
        ref = self.view(lane, dist, way)
        self.copy(ref, ref, lane, dist, way).wait_recv()


def kernel(
    x_hbm, wg_hbm, wu_hbm, wd_hbm, g_hbm,
    *refs,
):
    outs = refs[:5]
    (
        xall, gall, xsib, gsib, wg, wu, wd, wgs, wus, wds, pg, ph, pgf, phf,
        glanded, gtotal, ghalf, gother, hlanded, htotal, hhalf, hother, gu, hall, dall,
        po, pof, ro, so, zo, pi, pif, ri, si, zi, own, outv, ingv, ggv, ugv, dgv,
        lsem, wsend, wrecv, xs, xr, xps, xpr, gs, gr, gps, gpr, xss, xsr, gss, gsr,
        rgs, rgr, rhs, rhr, has, har, hbs, hbr, das, dar, dbs, dbr, hss, hsr, dss, dsr, ys, yr, zs, zr, rsem,
    ) = refs[5:]
    r = lax.axis_index("row")
    c = lax.axis_index("col")
    yh, x, k = r // 8, (r // 2) % 4, r % 2
    z, yl = c // 2, c % 2
    pending = []

    sibling = (yh * 8 + x * 2 + (1 - k), c)
    yl_partner = (r, z * 2 + (1 - yl))
    yh_partner = ((1 - yh) * 8 + x * 2 + k, c)

    def z_dev(d):
        return (r, lax.rem(z + d, 8) * 2 + yl)

    def z_next(way):
        return z_dev(1 if way == 0 else 7)

    def x_dev(d):
        return (yh * 8 + lax.rem(x + d, 4) * 2 + k, c)

    def x_next(way):
        return x_dev(1 if way == 0 else 3)

    def remote(src, dst, send, recv, device):
        return pltpu.make_async_remote_copy(
            src_ref=src, dst_ref=dst, send_sem=send, recv_sem=recv, device_id=device, device_id_type=MESH
        )

    def push(src, dst, send, recv, device):
        copy = remote(src, dst, send, recv, device)
        copy.start()
        pending.append(copy)

    local = [
        pltpu.make_async_copy(src, dst, lsem.at[i])
        for i, (src, dst) in enumerate((
            (x_hbm, xall.at[yl, 0]), (g_hbm, gall.at[yl, 0]), (wg_hbm, wg), (wu_hbm, wu), (wd_hbm, wd),
        ))
    ]
    for copy in local:
        copy.start()
    barrier = pltpu.get_barrier_semaphore()
    peers = [sibling, yl_partner, yh_partner] + [x_dev(d) for d in range(1, 4)] + [z_dev(d) for d in range(1, 8)]
    for peer in peers:
        pl.semaphore_signal(barrier, inc=1, device_id=peer, device_id_type=MESH)
    pl.semaphore_wait(barrier, len(peers))

    class Gather:
        def __init__(self, full, half, sems, pair_sems, swap_sems):
            def at(lane, dist, way):
                return full.at[yl if lane == 0 else 1 - yl, SLOT[(dist if way else 8 - dist) % 8]]

            self.full, self.half_tokens, self.pair_sems, self.swap_sems = full, half, pair_sems, swap_sems
            self.ring = Ring(4, at, at, at, lambda ref, way: ref.at[pl.ds(way * R, R)], z_next, sems, pending)

        def send_pair(self):
            ref = self.full.at[yl, 0]
            push(ref, ref, *self.pair_sems, yl_partner)

        def send_own(self):
            for way in (0, 1):
                self.ring.send(0, 1, way)

        def pair(self):
            ref = self.full.at[1 - yl, 0]
            remote(ref, ref, *self.pair_sems, yl_partner).wait_recv()
            for way in (0, 1):
                self.ring.send(1, 1, way)
            self.swap(0)

        def step(self, dist):
            for lane in (0, 1):
                for way in (0, 1):
                    self.ring.wait(lane, dist, way)
                    if dist < 4:
                        self.ring.send(lane, dist + 1, way)
            for d in sorted({dist, 8 - dist}):
                self.swap(SLOT[d])

        def swap(self, s):
            send, recv = self.swap_sems
            push(self.full.at[1 - k, s], self.half_tokens.at[s], send.at[s], recv.at[s], sibling)

        def swapped(self, chunk):
            send, recv = self.swap_sems
            for s in range(4 * chunk, 4 * chunk + 4):
                ref = self.half_tokens.at[s]
                remote(ref, ref, send.at[s], recv.at[s], sibling).wait_recv()

    gat_x = Gather(xall, xsib, (xs, xr), (xps, xpr), (xss, xsr))
    gat_g = Gather(gall, gsib, (gs, gr), (gps, gpr), (gss, gsr))

    def chunk_of(ref, chunk):
        return ref[pl.ds(4 * chunk, 4)].reshape(C, F)

    def put_partial(value, part, exact, chunk, col):
        value = value.reshape(2, 4, R, T)
        exact[chunk, :, :, :, pl.ds(col, T)] = value
        part[chunk, :, :, :, pl.ds(col, T)] = value.astype(BF16)

    def gate_up_sums(chunk):
        gat_x.swapped(chunk)
        for j, (w, ws) in enumerate(((wg, wgs), (wu, wus))):
            def tile(col, w=w, ws=ws, j=j):
                value = nn(chunk_of(xall.at[k], chunk), w[:, pl.ds(col, T)])
                value += nn(chunk_of(xsib, chunk), ws[:, pl.ds(col, T)])
                put_partial(value, pg, pgf, chunk, pl.multiple_of(j * H + col, T))

            tiles(H // T, tile)

    def hidden_grad_sums(chunk):
        gat_g.swapped(chunk)

        def tile(col):
            value = nt(chunk_of(gall.at[k], chunk), wd[pl.ds(col, T), :])
            value += nt(chunk_of(gsib, chunk), wds[pl.ds(col, T), :])
            put_partial(value, ph, phf, chunk, col)

        tiles(H // T, tile)

    class RowSum:
        def __init__(self, chunk, part, exact, landed, total, half, other, sems):
            self.part, self.exact, self.landed, self.total, self.half, self.other, self.send_sem, self.recv_sem = [
                ref.at[chunk] for ref in (part, exact, landed, total, half, other, *sems)
            ]

        def send(self):
            for d in (2, 1, 3):
                src = self.part.at[:, lax.rem(x + d, 4)]
                push(src, self.landed.at[d - 1], self.send_sem.at[d - 1], self.recv_sem.at[d - 1], x_dev(d))

        def arrived(self, ref, i):
            remote(ref, ref, self.send_sem.at[i], self.recv_sem.at[i], yh_partner).wait_recv()

        def pair(self):
            for d in range(3):
                self.arrived(self.landed.at[d], d)
            for lane in (0, 1):
                value = self.exact[lane, x]
                for d in range(3):
                    value += self.landed[d, lane].astype(F32)
                self.total[lane] = value
                self.half[lane] = value.astype(BF16)
            push(self.half, self.other, self.send_sem.at[3], self.recv_sem.at[3], yh_partner)

        def finish(self):
            self.arrived(self.other, 3)

        def value(self, lane, col):
            return self.total[lane, :, pl.ds(col, T)] + self.other[lane, :, pl.ds(col, T)].astype(F32)

    sum_gu = [RowSum(i, pg, pgf, glanded, gtotal, ghalf, gother, (rgs, rgr)) for i in (0, 1)]
    sum_h = [RowSum(i, ph, phf, hlanded, htotal, hhalf, hother, (rhs, rhr)) for i in (0, 1)]

    def hidden_of(chunk):
        sum_gu[chunk].finish()

        def tile(col):
            up_col = pl.multiple_of(H + col, T)
            for lane in (0, 1):
                gate, up = sum_gu[chunk].value(lane, col), sum_gu[chunk].value(lane, up_col)
                gu[chunk, lane, :, pl.ds(col, T)] = gate
                gu[chunk, lane, :, pl.ds(up_col, T)] = up
                hall[k, chunk, lane, x, :, pl.ds(col, T)] = (gate * jax.nn.sigmoid(gate) * up).astype(BF16)

        tiles(H // T, tile)

    def deltas_of(chunk):
        sum_h[chunk].finish()

        def tile(col):
            up_col = pl.multiple_of(H + col, T)
            for lane in (0, 1):
                hidden_grad = sum_h[chunk].value(lane, col)
                gate, up = gu[chunk, lane, :, pl.ds(col, T)], gu[chunk, lane, :, pl.ds(up_col, T)]
                sig = jax.nn.sigmoid(gate)
                dall[k, chunk, lane, x, :, pl.ds(up_col, T)] = (hidden_grad * (gate * sig)).astype(BF16)
                dall[k, chunk, lane, x, :, pl.ds(col, T)] = (
                    hidden_grad * up * sig * (1.0 + gate * (1.0 - sig))
                ).astype(BF16)

        tiles(H // T, tile)

    class RowGather:
        def __init__(self, full, chunk, sems, swap_sems):
            self.full, self.chunk, self.swap_sems = full, chunk, [sem.at[chunk] for sem in swap_sems]

            def src(lane, dist, way):
                return self.block(k, dist if way else 4 - dist)

            def dst(lane, dist, way):
                return src(lane, dist - 1, way)

            self.ring = Ring(2, src, dst, src, lambda ref, way: ref.at[way], x_next, sems, pending)

        def block(self, core, d):
            return self.full.at[core, self.chunk, :, lax.rem(x + d, 4)]

        def swap(self, d):
            ref = self.block(k, d)
            push(ref, ref, self.swap_sems[0].at[d], self.swap_sems[1].at[d], sibling)

        def start(self):
            for way in (0, 1):
                self.ring.send(0, 1, way)
            self.swap(0)

        def near(self):
            for way in (0, 1):
                self.ring.wait(0, 1, way)
                self.ring.send(0, 2, way)
                self.swap(1 if way else 3)

        def far(self):
            for way in (0, 1):
                self.ring.wait(0, 2, way)
            self.swap(2)

        def swapped(self):
            for d in range(4):
                ref = self.block(1 - k, d)
                remote(ref, ref, self.swap_sems[0].at[d], self.swap_sems[1].at[d], sibling).wait_recv()

    hid_a = RowGather(hall, 0, (has, har), (hss, hsr))
    hid_b = RowGather(hall, 1, (hbs, hbr), (hss, hsr))
    del_a = RowGather(dall, 0, (das, dar), (dss, dsr))
    del_b = RowGather(dall, 1, (dbs, dbr), (dss, dsr))

    class ColSum:
        def __init__(self, base, part, exact, received, summed, landed, result):
            self.base, self.part, self.exact, self.received = base, part, exact, received
            self.summed, self.landed, self.result = summed, landed, result

        def start(self, slots):
            for s in slots:
                push(self.part.at[s], self.received.at[s], ys.at[self.base, s], yr.at[self.base, s], yl_partner)

        def step(self, s):
            ref, d = self.received.at[s], NEAR[s]
            remote(ref, ref, ys.at[self.base, s], yr.at[self.base, s], yl_partner).wait_recv()
            total = self.exact[s] + self.received[s].astype(F32)
            if d == 0:
                own[self.base] = total
            else:
                self.summed[s] = total.astype(BF16)
                push(self.summed.at[s], self.landed.at[d - 1], zs.at[self.base, d - 1], zr.at[self.base, d - 1], z_dev(d))

        def finish(self):
            total = own[self.base]
            for d in (1, 7, 2, 6, 3, 5, 4):
                ref = self.landed.at[d - 1]
                remote(ref, ref, zs.at[self.base, d - 1], zr.at[self.base, d - 1], z_dev(d)).wait_recv()
            for d in range(7):
                total += self.landed[d].astype(F32)
            self.result[...] = total.astype(BF16)

    sum_out = ColSum(0, po, pof, ro, so, zo, outv)
    sum_ing = ColSum(1, pi, pif, ri, si, zi, ingv)

    def out_tile(half, chunk, col):
        return nn(hall[half, chunk].reshape(C, H), wd[:, pl.ds(col, T)])

    def ing_tile(half, chunk, col):
        left = dall[half, chunk].reshape(C, 2 * H)
        return nt(left[:, :H], wg[pl.ds(col, T), :]) + nt(left[:, H:], wu[pl.ds(col, T), :])

    def col_sums(total, tile, chunk, slots):
        def away(col):
            total.part[pl.ds(4 * chunk, 4), :, pl.ds(col, T)] = tile(1 - yl, chunk, col).astype(BF16).reshape(4, B, T)

        def home(col):
            total.exact[pl.ds(4 * chunk, 4), :, pl.ds(col, T)] = tile(yl, chunk, col).reshape(4, B, T)

        tiles(F // T, away)
        total.start(slots)
        tiles(F // T, home)

    def tokens(ref, col):
        return ref[:, :, :, :, :, pl.ds(col, T)].reshape(16 * B, T)

    def gate_grad_tile(col):
        ggv[:, pl.ds(col, T)] = tn(xall[...].reshape(16 * B, F), tokens(dall, col)).astype(BF16)

    def up_grad_tile(col):
        up_col = pl.multiple_of(H + col, T)
        ugv[:, pl.ds(col, T)] = tn(xall[...].reshape(16 * B, F), tokens(dall, up_col)).astype(BF16)

    def down_grad_tile(col):
        dgv[pl.ds(col, T), :] = tn(tokens(hall, col), gall[...].reshape(16 * B, F)).astype(BF16)

    results = [
        pltpu.make_async_copy(src, dst, rsem.at[i]) for i, (src, dst) in enumerate(zip((outv, ingv, ggv, ugv, dgv), outs))
    ]

    local[0].wait()
    gat_x.send_pair()
    gat_x.send_own()
    local[1].wait()
    gat_g.send_pair()
    for i, (src, dst) in enumerate(((wg, wgs), (wu, wus), (wd, wds))):
        local[2 + i].wait()
        push(src, dst, wsend.at[i], wrecv.at[i], sibling)
    gat_x.pair()
    gat_x.step(1)
    gat_g.send_own()
    gat_x.step(2)
    for i, dst in enumerate((wgs, wus, wds)):
        remote(dst, dst, wsend.at[i], wrecv.at[i], sibling).wait_recv()
    gat_g.pair()
    gate_up_sums(0)
    sum_gu[0].send()
    gat_x.step(3)
    gat_g.step(1)
    gat_x.step(4)
    gat_g.step(2)
    gate_up_sums(1)
    sum_gu[1].send()
    gat_g.step(3)
    sum_gu[0].pair()
    hidden_grad_sums(0)
    sum_h[0].send()
    gat_g.step(4)
    hidden_grad_sums(1)
    sum_h[1].send()
    hidden_of(0)
    hid_a.start()
    sum_gu[1].pair()
    sum_h[0].pair()
    hidden_of(1)
    hid_b.start()
    sum_h[1].pair()
    deltas_of(0)
    del_a.start()
    hid_a.near()
    deltas_of(1)
    del_b.start()
    hid_b.near()
    hid_a.far()
    del_a.near()
    hid_a.swapped()
    col_sums(sum_out, out_tile, 0, FAR_A)
    hid_b.far()
    del_b.near()
    hid_b.swapped()
    col_sums(sum_out, out_tile, 1, FAR_B)
    for s in FAR_A:
        sum_out.step(s)
    del_a.far()
    del_a.swapped()
    col_sums(sum_ing, ing_tile, 0, FAR_A)
    for s in FAR_B:
        sum_out.step(s)
    del_b.far()
    del_b.swapped()
    col_sums(sum_ing, ing_tile, 1, FAR_B)
    tiles(H // T, down_grad_tile)
    results[4].start()
    for s in FAR_A:
        sum_ing.step(s)
    tiles(H // T, gate_grad_tile)
    results[2].start()
    for s in FAR_B:
        sum_ing.step(s)
    tiles(H // T, up_grad_tile)
    results[3].start()
    sum_out.finish()
    results[0].start()
    sum_ing.finish()
    results[1].start()
    for copy in pending:
        copy.wait_send()
    for copy in results:
        copy.wait()


def deliver(*refs):
    sources, results, held, sems = refs[:5], refs[5:10], refs[10:15], refs[15]
    loads = [pltpu.make_async_copy(sources[i], held[i], sems.at[0, i]) for i in range(5)]
    stores = [pltpu.make_async_copy(held[i], results[i], sems.at[1, i]) for i in range(5)]
    for load in loads:
        load.start()
    for load, store in zip(loads, stores):
        load.wait()
        store.start()
    for store in stores:
        store.wait()


def body(inputs, gate_weight, up_weight, down_weight, out_grad):
    dma = pltpu.SemaphoreType.DMA
    shapes = tuple(jax.ShapeDtypeStruct(shape, BF16) for shape in ((B, F), (B, F), (F, H), (F, H), (H, F)))
    bf = lambda *shape: pltpu.VMEM(shape, BF16)
    f32 = lambda *shape: pltpu.VMEM(shape, F32)
    ring = lambda lanes, far: [dma((2, lanes, far))] * 2
    results = pl.pallas_call(
        kernel,
        out_shape=shapes,
        in_specs=[pl.BlockSpec(memory_space=pl.ANY)] * 5,
        out_specs=(pl.BlockSpec(memory_space=pl.ANY),) * 5,
        scratch_shapes=[
            bf(2, 8, B, F), bf(2, 8, B, F), bf(8, B, F), bf(8, B, F),
            bf(F, H), bf(F, H), bf(H, F), bf(F, H), bf(F, H), bf(H, F),
            bf(2, 2, 4, R, 2 * H), bf(2, 2, 4, R, H), f32(2, 2, 4, R, 2 * H), f32(2, 2, 4, R, H),
            bf(2, 3, 2, R, 2 * H), f32(2, 2, R, 2 * H), bf(2, 2, R, 2 * H), bf(2, 2, R, 2 * H),
            bf(2, 3, 2, R, H), f32(2, 2, R, H), bf(2, 2, R, H), bf(2, 2, R, H),
            f32(2, 2, R, 2 * H), bf(2, 2, 2, 4, R, H), bf(2, 2, 2, 4, R, 2 * H),
            bf(8, B, F), f32(8, B, F), bf(8, B, F), bf(8, B, F), bf(7, B, F),
            bf(8, B, F), f32(8, B, F), bf(8, B, F), bf(8, B, F), bf(7, B, F),
            f32(2, B, F), bf(B, F), bf(B, F), bf(F, H), bf(F, H), bf(H, F),
            dma((5,)), dma((3,)), dma((3,)),
            *ring(2, 4), dma, dma, *ring(2, 4), dma, dma,
            dma((8,)), dma((8,)), dma((8,)), dma((8,)),
            dma((2, 4)), dma((2, 4)), dma((2, 4)), dma((2, 4)),
            *ring(1, 2), *ring(1, 2), *ring(1, 2), *ring(1, 2),
            dma((2, 4)), dma((2, 4)), dma((2, 4)), dma((2, 4)),
            dma((2, 8)), dma((2, 8)), dma((2, 7)), dma((2, 7)), dma((5,)),
        ],
        compiler_params=pltpu.CompilerParams(collective_id=0, has_side_effects=True, vmem_limit_bytes=60 << 20),
        name="ffn",
    )(inputs, gate_weight, up_weight, down_weight, out_grad)
    return pl.pallas_call(
        deliver,
        out_shape=shapes,
        in_specs=[pl.BlockSpec(memory_space=pl.ANY)] * 5,
        out_specs=(pl.BlockSpec(memory_space=pl.ANY),) * 5,
        scratch_shapes=[*[pltpu.VMEM(shape.shape, BF16) for shape in shapes], dma((2, 5))],
        name="deliver",
    )(*results)


def solution(mesh):
    return jax.shard_map(
        body,
        mesh=mesh,
        in_specs=(P("col", "row"), P("row", "col"), P("row", "col"), P("col", "row"), P("col", "row")),
        out_specs=(P("col", "row"), P("col", "row"), P("row", "col"), P("row", "col"), P("col", "row")),
        check_vma=False,
    )
```

time: 664 us -> 104 us (0.16); the launches traced: 653 us -> 104 us
  waiting for transfers between devices: 592 us -> 0 us
  Pallas kernels: 0 us -> 104 us
  matrix products: 26.3 us -> 0 us
  between operations: 13.9 us -> 0.64 us
  local copies, waits for them, and re-layouts: 12.8 us -> 0 us
  other arithmetic: 8.18 us -> 0 us
    reduce_scatter x4 -> x0, waiting for transfers between devices: 306 us -> none  [the longest x1 100 us: body(): lax.psum_scatter(jnp.concatenate([gate_part, up_part], axis=1), 'row', sc...]
    all_gather x5 -> x0, waiting for transfers between devices: 282 us -> none  [the longest x1 67.1 us: body(): inputs_all = lax.all_gather(inputs, 'col', axis=0, tiled=True)]
    pallas_call x0 -> x2, Pallas kernels: none -> 104 us  [the longest x1 101 us: body(): pl.pallas_call(kernel, out_shape=shapes, in_specs=[pl.BlockSpec(memory_sp...]
    dot_general x8 -> x0, matrix products: 22.2 us -> none  [the longest x2 8.09 us: contract_last(): lax.dot_general(left, right, (((1,), (1,)), ((), ())), preferred_element_...]
    unnamed x17 -> x0, local copies, waits for them, and re-layouts: 12.8 us -> none
  transfers between devices with their start and end apart: 9 -> 0, of which waited for: 9 -> 0; matrix products, arithmetic and copies ran while one was open for 6% -> 0% of each run, Pallas kernels for 0% -> 0%
where the time goes in v2:
time: 104 us
  Pallas kernels  104 us (100%)
    pallas_call x1, Pallas kernels, body(): pl.pallas_call(kernel, out_shape=shapes, in_specs=[pl.BlockSpec(memory_sp...  101 us
    pallas_call x1, Pallas kernels, body(): pl.pallas_call(deliver, out_shape=shapes, in_specs=[pl.BlockSpec(memory_s...  2.7 us

profile of v2, /device:TPU:1, one launch (start us, length us, event | category | flops | bytes accessed | tf_op | source)
XLA Modules:
  0.0 104.3 jit_solution(6304749997301489853)
XLA Ops:
  0.6 101.0 %ffn.1 = (bf16[64,512]{1,0:T(8,128)(2,1)}, bf16[64,512]{1,0:T(8,128)(2,1)}, bf16[512,768]{1,0:T(8,128)(2,1)}, bf16[512,768]{1,0:T(8,128)(2,1)}, bf16[768,512]{1,0:T(8,128)(2,1)}) custom-call(bf16[64,512]{1,0:T(8,128)(2,1)} %x_hbm.1, bf16[512,768]{1,0:T(8,128)(2,1)} %wg_hbm.1, bf16[512,768]{1,0:T(8,128)(2,1)} %wu_hbm.1, bf16[768,512]{1,0:T(8,128)(2,1)} %wd_hbm.1, ...), custom_call_target="tpu_custom_call" | custom-call | tf_op jit(solution)/shard_map/ffn/pallas_call | solution.py:472
  101.6 2.7 %deliver.1 = (bf16[64,512]{1,0:T(8,128)(2,1)}, bf16[64,512]{1,0:T(8,128)(2,1)}, bf16[512,768]{1,0:T(8,128)(2,1)}, bf16[512,768]{1,0:T(8,128)(2,1)}, bf16[768,512]{1,0:T(8,128)(2,1)}) custom-call(bf16[64,512]{1,0:T(8,128)(2,1)} %get-tuple-element.10.refs_0_, bf16[64,512]{1,0:T(8,128)(2,1)} %get-tuple-element.11.refs_1_, ...), custom_call_target="tpu_custom_call" | custom-call | tf_op jit(solution)/shard_map/deliver/pallas_call | solution.py:498

commit v3 on v2

v3 whole, which is shorter than its diff:
```python
import jax
import jax.numpy as jnp
from jax import lax
from jax.experimental import pallas as pl
from jax.experimental.pallas import tpu as pltpu
from jax.sharding import PartitionSpec as P

MESH = pl.DeviceIdType.MESH
F32 = jnp.float32
BF16 = jnp.bfloat16
B = 64
F = 512
H = 768
T = 256
NEAR = (0, 1, 7, 2, 6, 3, 5, 4)
SLOT = tuple(NEAR.index(d) for d in range(8))
N = 4
S = 8 // N
C = S * B
R = C // 8
POOL = 48


def nn(left, right):
    return jnp.dot(left, right, preferred_element_type=F32)


def nt(left, right):
    return lax.dot_general(left, right, (((1,), (1,)), ((), ())), preferred_element_type=F32)


def tn(left, right):
    return lax.dot_general(left, right, (((0,), (0,)), ((), ())), preferred_element_type=F32)


def tiles(count, body):
    def step(i, carry):
        body(pl.multiple_of(i * T, T))
        return carry

    lax.fori_loop(0, count, step, 0)


class Ring:
    def __init__(self, far, src, dst, view, half, neighbour, sems, push, wait_for):
        self.far, self.src, self.dst, self.view, self.half = far, src, dst, view, half
        self.neighbour, self.sems, self.push, self.wait_for = neighbour, sems, push, wait_for

    def part(self, ref, dist, way):
        return self.half(ref, way) if dist == self.far else ref

    def send(self, lane, dist, way):
        src, dst = [self.part(ref, dist, way) for ref in (self.src(lane, dist - 1, way), self.dst(lane, dist, way))]
        self.push(src, dst, self.sems.at[way, lane, dist - 1], self.neighbour(way))

    def wait(self, lane, dist, way):
        self.wait_for(self.part(self.view(lane, dist, way), dist, way), self.sems.at[way, lane, dist - 1])


def kernel(
    x_hbm, wg_hbm, wu_hbm, wd_hbm, g_hbm,
    *refs,
):
    outs = refs[:5]
    (
        xall, gall, xsib, gsib, wg, wu, wd, wgs, wus, wds, pg, ph, pgf, phf,
        glanded, gtotal, ghalf, gother, hlanded, htotal, hhalf, hother, gu, hall, dall,
        po, pof, ro, so, zo, pi, pif, ri, si, zi, own, outv, ingv, ggv, ugv, dgv,
        lsem, pool, wrecv, xr, xpr, gr, gpr, xsr, gsr, rgr, rhr, hr, dr, hsr, dsr, yr, zr, rsem,
    ) = refs[5:]
    r = lax.axis_index("row")
    c = lax.axis_index("col")
    yh, x, k = r // 8, (r // 2) % 4, r % 2
    z, yl = c // 2, c % 2
    pending = []

    sibling = (yh * 8 + x * 2 + (1 - k), c)
    yl_partner = (r, z * 2 + (1 - yl))
    yh_partner = ((1 - yh) * 8 + x * 2 + k, c)

    def z_dev(d):
        return (r, lax.rem(z + d, 8) * 2 + yl)

    def z_next(way):
        return z_dev(1 if way == 0 else 7)

    def x_dev(d):
        return (yh * 8 + lax.rem(x + d, 4) * 2 + k, c)

    def x_next(way):
        return x_dev(1 if way == 0 else 3)

    def push(src, dst, recv, device):
        count = len(pending)
        if count >= POOL:
            pending[count - POOL].wait_send()
        copy = pltpu.make_async_remote_copy(
            src_ref=src, dst_ref=dst, send_sem=pool.at[count % POOL], recv_sem=recv,
            device_id=device, device_id_type=MESH,
        )
        copy.start()
        pending.append(copy)

    def wait_for(ref, recv):
        pltpu.make_async_remote_copy(
            src_ref=ref, dst_ref=ref, send_sem=pool.at[0], recv_sem=recv, device_id=sibling, device_id_type=MESH
        ).wait_recv()

    local = [
        pltpu.make_async_copy(src, dst, lsem.at[i])
        for i, (src, dst) in enumerate((
            (x_hbm, xall.at[yl, 0]), (g_hbm, gall.at[yl, 0]), (wg_hbm, wg), (wu_hbm, wu), (wd_hbm, wd),
        ))
    ]
    for copy in local:
        copy.start()
    barrier = pltpu.get_barrier_semaphore()
    peers = [sibling, yl_partner, yh_partner] + [x_dev(d) for d in range(1, 4)] + [z_dev(d) for d in range(1, 8)]
    for peer in peers:
        pl.semaphore_signal(barrier, inc=1, device_id=peer, device_id_type=MESH)
    pl.semaphore_wait(barrier, len(peers))

    def half_rows(ref, way):
        return ref.at[pl.ds(way * (B // 2), B // 2)]

    class Gather:
        def __init__(self, full, half, recv, pair_recv, swap_recv):
            def at(lane, dist, way):
                return full.at[yl if lane == 0 else 1 - yl, SLOT[(dist if way else 8 - dist) % 8]]

            self.full, self.half_tokens, self.pair_recv, self.swap_recv = full, half, pair_recv, swap_recv
            self.ring = Ring(4, at, at, at, half_rows, z_next, recv, push, wait_for)

        def send_pair(self):
            ref = self.full.at[yl, 0]
            push(ref, ref, self.pair_recv, yl_partner)

        def send_own(self):
            for way in (0, 1):
                self.ring.send(0, 1, way)

        def pair(self):
            ref = self.full.at[1 - yl, 0]
            wait_for(ref, self.pair_recv)
            for way in (0, 1):
                self.ring.send(1, 1, way)
            self.swap(0)

        def step(self, dist):
            for lane in (0, 1):
                for way in (0, 1):
                    self.ring.wait(lane, dist, way)
                    if dist < 4:
                        self.ring.send(lane, dist + 1, way)
            for d in sorted({dist, 8 - dist}):
                self.swap(SLOT[d])

        def swap(self, s):
            push(self.full.at[1 - k, s], self.half_tokens.at[s], self.swap_recv.at[s // S], sibling)

        def swapped(self, chunk):
            wait_for(self.half_tokens.at[pl.ds(S * chunk, S)], self.swap_recv.at[chunk])

    gat_x = Gather(xall, xsib, xr, xpr, xsr)
    gat_g = Gather(gall, gsib, gr, gpr, gsr)

    def chunk_of(ref, chunk):
        return ref[pl.ds(S * chunk, S)].reshape(C, F)

    def put_partial(value, part, exact, chunk, col):
        value = value.reshape(2, 4, R, T)
        exact[chunk, :, :, :, pl.ds(col, T)] = value
        part[chunk, :, :, :, pl.ds(col, T)] = value.astype(BF16)

    def gate_up_sums(chunk):
        gat_x.swapped(chunk)
        for j, (w, ws) in enumerate(((wg, wgs), (wu, wus))):
            def tile(col, w=w, ws=ws, j=j):
                value = nn(chunk_of(xall.at[k], chunk), w[:, pl.ds(col, T)])
                value += nn(chunk_of(xsib, chunk), ws[:, pl.ds(col, T)])
                put_partial(value, pg, pgf, chunk, pl.multiple_of(j * H + col, T))

            tiles(H // T, tile)

    def hidden_grad_sums(chunk):
        gat_g.swapped(chunk)

        def tile(col):
            value = nt(chunk_of(gall.at[k], chunk), wd[pl.ds(col, T), :])
            value += nt(chunk_of(gsib, chunk), wds[pl.ds(col, T), :])
            put_partial(value, ph, phf, chunk, col)

        tiles(H // T, tile)

    class RowSum:
        def __init__(self, chunk, part, exact, landed, total, half, other, recv):
            self.part, self.exact, self.landed, self.total, self.half, self.other, self.recv = [
                ref.at[chunk] for ref in (part, exact, landed, total, half, other, recv)
            ]

        def send(self):
            for d in (2, 1, 3):
                src = self.part.at[:, lax.rem(x + d, 4)]
                push(src, self.landed.at[d - 1], self.recv.at[0], x_dev(d))

        def pair(self):
            wait_for(self.landed, self.recv.at[0])
            for lane in (0, 1):
                value = self.exact[lane, x]
                for d in range(3):
                    value += self.landed[d, lane].astype(F32)
                self.total[lane] = value
                self.half[lane] = value.astype(BF16)
            push(self.half, self.other, self.recv.at[1], yh_partner)

        def finish(self):
            wait_for(self.other, self.recv.at[1])

        def value(self, lane, col):
            return self.total[lane, :, pl.ds(col, T)] + self.other[lane, :, pl.ds(col, T)].astype(F32)

    sum_gu = [RowSum(i, pg, pgf, glanded, gtotal, ghalf, gother, rgr) for i in range(N)]
    sum_h = [RowSum(i, ph, phf, hlanded, htotal, hhalf, hother, rhr) for i in range(N)]

    def gate_up(chunk):
        gate_up_sums(chunk)
        sum_gu[chunk].send()

    def hidden_grad(chunk):
        hidden_grad_sums(chunk)
        sum_h[chunk].send()

    def hidden_of(chunk):
        sum_gu[chunk].finish()

        def tile(col):
            up_col = pl.multiple_of(H + col, T)
            for lane in (0, 1):
                gate, up = sum_gu[chunk].value(lane, col), sum_gu[chunk].value(lane, up_col)
                gu[chunk, lane, :, pl.ds(col, T)] = gate
                gu[chunk, lane, :, pl.ds(up_col, T)] = up
                hall[k, chunk, lane, x, :, pl.ds(col, T)] = (gate * jax.nn.sigmoid(gate) * up).astype(BF16)

        tiles(H // T, tile)
        hid[chunk].start()

    def deltas_of(chunk):
        sum_h[chunk].finish()

        def tile(col):
            up_col = pl.multiple_of(H + col, T)
            for lane in (0, 1):
                hidden_grad = sum_h[chunk].value(lane, col)
                gate, up = gu[chunk, lane, :, pl.ds(col, T)], gu[chunk, lane, :, pl.ds(up_col, T)]
                sig = jax.nn.sigmoid(gate)
                dall[k, chunk, lane, x, :, pl.ds(up_col, T)] = (hidden_grad * (gate * sig)).astype(BF16)
                dall[k, chunk, lane, x, :, pl.ds(col, T)] = (
                    hidden_grad * up * sig * (1.0 + gate * (1.0 - sig))
                ).astype(BF16)

        tiles(H // T, tile)
        delta[chunk].start()

    class RowGather:
        def __init__(self, full, chunk, recv, swap_recv, straight):
            self.full, self.chunk, self.straight = full, chunk, straight
            self.far_recv, self.swap_recv = recv.at[0, 0, 1], swap_recv.at[chunk]

            def src(lane, dist, way):
                return self.block(k, dist if way else 4 - dist)

            def dst(lane, dist, way):
                return src(lane, dist - 1, way)

            self.ring = Ring(2, src, dst, src, lambda ref, way: ref.at[way], x_next, recv, push, wait_for)

        def block(self, core, d):
            return self.full.at[core, self.chunk, :, lax.rem(x + d, 4)]

        def swap(self, d):
            ref = self.block(k, d)
            push(ref, ref, self.swap_recv, sibling)

        def start(self):
            for way in (0, 1):
                self.ring.send(0, 1, way)
            if self.straight:
                push(self.block(k, 0), self.block(k, 0), self.far_recv, x_dev(2))
            self.swap(0)

        def near(self):
            for way in (0, 1):
                self.ring.wait(0, 1, way)
                if not self.straight:
                    self.ring.send(0, 2, way)
                self.swap(1 if way else 3)

        def far(self):
            if self.straight:
                wait_for(self.block(k, 2), self.far_recv)
            else:
                for way in (0, 1):
                    self.ring.wait(0, 2, way)
            self.swap(2)

        def swapped(self):
            wait_for(self.full.at[1 - k, self.chunk], self.swap_recv)

    hid = [RowGather(hall, i, hr.at[i], hsr, True) for i in range(N)]
    delta = [RowGather(dall, i, dr.at[i], dsr, False) for i in range(N)]

    class ColSum:
        def __init__(self, base, part, exact, received, summed, landed, result):
            self.base, self.part, self.exact, self.received = base, part, exact, received
            self.summed, self.landed, self.result = summed, landed, result

        def start(self, chunk):
            for s in reversed(range(S * chunk, S * chunk + S)):
                push(self.part.at[1 - yl, s], self.received.at[s], yr.at[self.base, s], yl_partner)

        def steps(self, chunk):
            for s in reversed(range(S * chunk, S * chunk + S)):
                self.step(s)

        def step(self, s):
            d = NEAR[s]
            wait_for(self.received.at[s], yr.at[self.base, s])
            total = self.exact[yl, s] + self.received[s].astype(F32)
            if d == 0:
                own[self.base] = total
            else:
                self.summed[s] = total.astype(BF16)
                push(self.summed.at[s], self.landed.at[d - 1], zr.at[self.base], z_dev(d))

        def finish(self):
            total = own[self.base]
            wait_for(self.landed, zr.at[self.base])
            for d in range(7):
                total += self.landed[d].astype(F32)
            self.result[...] = total.astype(BF16)

    sum_out = ColSum(0, po, pof, ro, so, zo, outv)
    sum_ing = ColSum(1, pi, pif, ri, si, zi, ingv)

    def out_tile(chunk, col):
        return nn(hall[:, chunk].reshape(2 * C, H), wd[:, pl.ds(col, T)])

    def ing_tile(chunk, col):
        left = dall[:, chunk].reshape(2 * C, 2 * H)
        return nt(left[:, :H], wg[pl.ds(col, T), :]) + nt(left[:, H:], wu[pl.ds(col, T), :])

    def col_sums(total, tile, chunk):
        slots = pl.ds(S * chunk, S)

        def both(col):
            value = tile(chunk, col).reshape(2, S, B, T)
            total.exact[:, slots, :, pl.ds(col, T)] = value
            total.part[:, slots, :, pl.ds(col, T)] = value.astype(BF16)

        tiles(F // T, both)
        total.start(chunk)

    def out_sums(chunk):
        hid[chunk].swapped()
        col_sums(sum_out, out_tile, chunk)

    def ing_sums(chunk):
        delta[chunk].swapped()
        col_sums(sum_ing, ing_tile, chunk)

    def tokens(ref, col):
        return ref[:, :, :, :, :, pl.ds(col, T)].reshape(16 * B, T)

    def gate_grad_tile(col):
        ggv[:, pl.ds(col, T)] = tn(xall[...].reshape(16 * B, F), tokens(dall, col)).astype(BF16)

    def up_grad_tile(col):
        up_col = pl.multiple_of(H + col, T)
        ugv[:, pl.ds(col, T)] = tn(xall[...].reshape(16 * B, F), tokens(dall, up_col)).astype(BF16)

    def down_grad_tile(col):
        dgv[pl.ds(col, T), :] = tn(tokens(hall, col), gall[...].reshape(16 * B, F)).astype(BF16)

    results = [
        pltpu.make_async_copy(src, dst, rsem.at[i]) for i, (src, dst) in enumerate(zip((outv, ingv, ggv, ugv, dgv), outs))
    ]

    local[0].wait()
    gat_x.send_pair()
    gat_x.send_own()
    local[1].wait()
    gat_g.send_pair()
    for i, (src, dst) in enumerate(((wg, wgs), (wu, wus), (wd, wds))):
        local[2 + i].wait()
        push(src, dst, wrecv.at[i], sibling)
    gat_x.pair()
    gat_x.step(1)
    gat_g.send_own()
    for i, dst in enumerate((wgs, wus, wds)):
        wait_for(dst, wrecv.at[i])
    gate_up(0)
    gat_x.step(2)
    gat_g.pair()
    gate_up(1)
    gat_x.step(3)
    gat_g.step(1)
    sum_gu[0].pair()
    gate_up(2)
    gat_x.step(4)
    gat_g.step(2)
    sum_gu[1].pair()
    hidden_of(0)
    gate_up(3)
    gat_g.step(3)
    sum_gu[2].pair()
    hidden_of(1)
    gat_g.step(4)
    hidden_grad(3)
    hid[0].near()
    hid[0].far()
    hidden_of(2)
    hidden_grad(2)
    sum_gu[3].pair()
    hidden_grad(1)
    sum_h[3].pair()
    out_sums(0)
    hid[1].near()
    hid[1].far()
    hidden_of(3)
    hidden_grad(0)
    sum_h[2].pair()
    deltas_of(3)
    out_sums(1)
    hid[2].near()
    hid[2].far()
    sum_out.steps(0)
    sum_h[1].pair()
    deltas_of(2)
    out_sums(2)
    hid[3].near()
    hid[3].far()
    sum_h[0].pair()
    sum_out.steps(1)
    out_sums(3)
    delta[3].near()
    deltas_of(1)
    sum_out.steps(2)
    delta[2].near()
    deltas_of(0)
    sum_out.steps(3)
    delta[3].far()
    delta[1].near()
    ing_sums(3)
    delta[2].far()
    delta[0].near()
    ing_sums(2)
    sum_ing.steps(3)
    delta[1].far()
    delta[0].far()
    ing_sums(1)
    ing_sums(0)
    sum_ing.steps(2)
    tiles(H // T, down_grad_tile)
    results[4].start()
    sum_ing.steps(1)
    tiles(H // T, gate_grad_tile)
    results[2].start()
    sum_ing.steps(0)
    tiles(H // T, up_grad_tile)
    results[3].start()
    sum_out.finish()
    results[0].start()
    sum_ing.finish()
    results[1].start()
    for copy in pending[-POOL:]:
        copy.wait_send()
    for copy in results:
        copy.wait()


def deliver(*refs):
    sources, results, held, sems = refs[:5], refs[5:10], refs[10:15], refs[15]
    loads = [pltpu.make_async_copy(sources[i], held[i], sems.at[0, i]) for i in range(5)]
    stores = [pltpu.make_async_copy(held[i], results[i], sems.at[1, i]) for i in range(5)]
    for load in loads:
        load.start()
    for load, store in zip(loads, stores):
        load.wait()
        store.start()
    for store in stores:
        store.wait()


def body(inputs, gate_weight, up_weight, down_weight, out_grad):
    dma = pltpu.SemaphoreType.DMA
    shapes = tuple(jax.ShapeDtypeStruct(shape, BF16) for shape in ((B, F), (B, F), (F, H), (F, H), (H, F)))
    bf = lambda *shape: pltpu.VMEM(shape, BF16)
    f32 = lambda *shape: pltpu.VMEM(shape, F32)
    results = pl.pallas_call(
        kernel,
        out_shape=shapes,
        in_specs=[pl.BlockSpec(memory_space=pl.ANY)] * 5,
        out_specs=(pl.BlockSpec(memory_space=pl.ANY),) * 5,
        scratch_shapes=[
            bf(2, 8, B, F), bf(2, 8, B, F), bf(8, B, F), bf(8, B, F),
            bf(F, H), bf(F, H), bf(H, F), bf(F, H), bf(F, H), bf(H, F),
            bf(N, 2, 4, R, 2 * H), bf(N, 2, 4, R, H), f32(N, 2, 4, R, 2 * H), f32(N, 2, 4, R, H),
            bf(N, 3, 2, R, 2 * H), f32(N, 2, R, 2 * H), bf(N, 2, R, 2 * H), bf(N, 2, R, 2 * H),
            bf(N, 3, 2, R, H), f32(N, 2, R, H), bf(N, 2, R, H), bf(N, 2, R, H),
            f32(N, 2, R, 2 * H), bf(2, N, 2, 4, R, H), bf(2, N, 2, 4, R, 2 * H),
            bf(2, 8, B, F), f32(2, 8, B, F), bf(8, B, F), bf(8, B, F), bf(7, B, F),
            bf(2, 8, B, F), f32(2, 8, B, F), bf(8, B, F), bf(8, B, F), bf(7, B, F),
            f32(2, B, F), bf(B, F), bf(B, F), bf(F, H), bf(F, H), bf(H, F),
            dma((5,)), dma((POOL,)), dma((3,)),
            dma((2, 2, 4)), dma, dma((2, 2, 4)), dma, dma((N,)), dma((N,)),
            dma((N, 2)), dma((N, 2)), dma((N, 2, 1, 2)), dma((N, 2, 1, 2)), dma((N,)), dma((N,)),
            dma((2, 8)), dma((2,)), dma((5,)),
        ],
        compiler_params=pltpu.CompilerParams(collective_id=0, has_side_effects=True, vmem_limit_bytes=60 << 20),
        name="ffn",
    )(inputs, gate_weight, up_weight, down_weight, out_grad)
    return pl.pallas_call(
        deliver,
        out_shape=shapes,
        in_specs=[pl.BlockSpec(memory_space=pl.ANY)] * 5,
        out_specs=(pl.BlockSpec(memory_space=pl.ANY),) * 5,
        scratch_shapes=[*[pltpu.VMEM(shape.shape, BF16) for shape in shapes], dma((2, 5))],
        name="deliver",
    )(*results)


def solution(mesh):
    return jax.shard_map(
        body,
        mesh=mesh,
        in_specs=(P("col", "row"), P("row", "col"), P("row", "col"), P("col", "row"), P("col", "row")),
        out_specs=(P("col", "row"), P("col", "row"), P("row", "col"), P("row", "col"), P("col", "row")),
        check_vma=False,
    )
```

time: 104 us -> 90 us (0.87)
  Pallas kernels: 104 us -> 89.2 us
    pallas_call x1, Pallas kernels: 101 us -> 86.5 us  [body(): pl.pallas_call(kernel, out_shape=shapes, in_specs=[pl.BlockSpec(memory_sp...]
where the time goes in v3:
time: 90 us; the launch traced here: 89.8 us
  Pallas kernels  89.2 us (99%)
    pallas_call x1, Pallas kernels, body(): pl.pallas_call(kernel, out_shape=shapes, in_specs=[pl.BlockSpec(memory_sp...  86.5 us
    pallas_call x1, Pallas kernels, body(): pl.pallas_call(deliver, out_shape=shapes, in_specs=[pl.BlockSpec(memory_s...  2.7 us

profile of v3, /device:TPU:1, one launch (start us, length us, event | category | flops | bytes accessed | tf_op | source)
XLA Modules:
  0.0 89.8 jit_solution(976836866773207158)
XLA Ops:
  0.6 86.5 %ffn.1 = (bf16[64,512]{1,0:T(8,128)(2,1)}, bf16[64,512]{1,0:T(8,128)(2,1)}, bf16[512,768]{1,0:T(8,128)(2,1)}, bf16[512,768]{1,0:T(8,128)(2,1)}, bf16[768,512]{1,0:T(8,128)(2,1)}) custom-call(bf16[64,512]{1,0:T(8,128)(2,1)} %x_hbm.1, bf16[512,768]{1,0:T(8,128)(2,1)} %wg_hbm.1, bf16[512,768]{1,0:T(8,128)(2,1)} %wu_hbm.1, bf16[768,512]{1,0:T(8,128)(2,1)} %wd_hbm.1, ...), custom_call_target="tpu_custom_call" | custom-call | tf_op jit(solution)/shard_map/ffn/pallas_call | solution.py:499
  87.1 2.7 %deliver.1 = (bf16[64,512]{1,0:T(8,128)(2,1)}, bf16[64,512]{1,0:T(8,128)(2,1)}, bf16[512,768]{1,0:T(8,128)(2,1)}, bf16[512,768]{1,0:T(8,128)(2,1)}, bf16[768,512]{1,0:T(8,128)(2,1)}) custom-call(bf16[64,512]{1,0:T(8,128)(2,1)} %get-tuple-element.10.refs_0_, bf16[64,512]{1,0:T(8,128)(2,1)} %get-tuple-element.11.refs_1_, ...), custom_call_target="tpu_custom_call" | custom-call | tf_op jit(solution)/shard_map/deliver/pallas_call | solution.py:522

commit v4 on v3

--- a/solution.py
+++ b/solution.py
@@ -19,6 +19,8 @@
 C = S * B
 R = C // 8
 POOL = 48
+HID_STRAIGHT = (False, False, False, True)
+DELTA_STRAIGHT = (True, False, True, True)
 
 
 def nn(left, right):
@@ -172,15 +174,15 @@
         exact[chunk, :, :, :, pl.ds(col, T)] = value
         part[chunk, :, :, :, pl.ds(col, T)] = value.astype(BF16)
 
-    def gate_up_sums(chunk):
-        gat_x.swapped(chunk)
-        for j, (w, ws) in enumerate(((wg, wgs), (wu, wus))):
-            def tile(col, w=w, ws=ws, j=j):
-                value = nn(chunk_of(xall.at[k], chunk), w[:, pl.ds(col, T)])
-                value += nn(chunk_of(xsib, chunk), ws[:, pl.ds(col, T)])
-                put_partial(value, pg, pgf, chunk, pl.multiple_of(j * H + col, T))
-
-            tiles(H // T, tile)
+    def half_sums(chunk, j):
+        w, ws = ((wg, wgs), (wu, wus))[j]
+
+        def tile(col):
+            value = nn(chunk_of(xall.at[k], chunk), w[:, pl.ds(col, T)])
+            value += nn(chunk_of(xsib, chunk), ws[:, pl.ds(col, T)])
+            put_partial(value, pg, pgf, chunk, pl.multiple_of(j * H + col, T))
+
+        tiles(H // T, tile)
 
     def hidden_grad_sums(chunk):
         gat_g.swapped(chunk)
@@ -198,10 +200,11 @@
                 ref.at[chunk] for ref in (part, exact, landed, total, half, other, recv)
             ]
 
-        def send(self):
+        def send(self, first):
+            cols = pl.ds(first, H)
             for d in (2, 1, 3):
-                src = self.part.at[:, lax.rem(x + d, 4)]
-                push(src, self.landed.at[d - 1], self.recv.at[0], x_dev(d))
+                src = self.part.at[:, lax.rem(x + d, 4), :, cols]
+                push(src, self.landed.at[d - 1, :, :, cols], self.recv.at[0], x_dev(d))
 
         def pair(self):
             wait_for(self.landed, self.recv.at[0])
@@ -222,13 +225,18 @@
     sum_gu = [RowSum(i, pg, pgf, glanded, gtotal, ghalf, gother, rgr) for i in range(N)]
     sum_h = [RowSum(i, ph, phf, hlanded, htotal, hhalf, hother, rhr) for i in range(N)]
 
-    def gate_up(chunk):
-        gate_up_sums(chunk)
-        sum_gu[chunk].send()
+    def gate_part(chunk):
+        gat_x.swapped(chunk)
+        half_sums(chunk, 0)
+        sum_gu[chunk].send(0)
+
+    def up_part(chunk):
+        half_sums(chunk, 1)
+        sum_gu[chunk].send(H)
 
     def hidden_grad(chunk):
         hidden_grad_sums(chunk)
-        sum_h[chunk].send()
+        sum_h[chunk].send(0)
 
     def hidden_of(chunk):
         sum_gu[chunk].finish()
@@ -306,8 +314,8 @@
         def swapped(self):
             wait_for(self.full.at[1 - k, self.chunk], self.swap_recv)
 
-    hid = [RowGather(hall, i, hr.at[i], hsr, True) for i in range(N)]
-    delta = [RowGather(dall, i, dr.at[i], dsr, False) for i in range(N)]
+    hid = [RowGather(hall, i, hr.at[i], hsr, HID_STRAIGHT[i]) for i in range(N)]
+    delta = [RowGather(dall, i, dr.at[i], dsr, DELTA_STRAIGHT[i]) for i in range(N)]
 
     class ColSum:
         def __init__(self, base, part, exact, received, summed, landed, result):
@@ -394,82 +402,94 @@
         local[2 + i].wait()
         push(src, dst, wrecv.at[i], sibling)
     gat_x.pair()
+    gat_g.send_own()
     gat_x.step(1)
-    gat_g.send_own()
+    gat_g.pair()
     for i, dst in enumerate((wgs, wus, wds)):
         wait_for(dst, wrecv.at[i])
-    gate_up(0)
+    gate_part(0)
+    up_part(0)
     gat_x.step(2)
-    gat_g.pair()
-    gate_up(1)
+    gate_part(1)
+    up_part(1)
+    gat_g.step(1)
     gat_x.step(3)
-    gat_g.step(1)
-    sum_gu[0].pair()
-    gate_up(2)
-    gat_x.step(4)
+    gate_part(2)
+    up_part(2)
     gat_g.step(2)
     sum_gu[1].pair()
-    hidden_of(0)
-    gate_up(3)
+    sum_gu[0].pair()
+    gat_x.step(4)
+    gate_part(3)
+    up_part(3)
+    hidden_of(1)
+    sum_gu[2].pair()
+    hidden_grad(1)
     gat_g.step(3)
-    sum_gu[2].pair()
-    hidden_of(1)
-    gat_g.step(4)
-    hidden_grad(3)
-    hid[0].near()
-    hid[0].far()
-    hidden_of(2)
     hidden_grad(2)
     sum_gu[3].pair()
-    hidden_grad(1)
-    sum_h[3].pair()
-    out_sums(0)
     hid[1].near()
+    gat_g.step(4)
+    hidden_of(2)
+    hidden_of(3)
+    hidden_grad(3)
     hid[1].far()
-    hidden_of(3)
-    hidden_grad(0)
+    hidden_of(0)
+    sum_h[1].pair()
+    hid[2].near()
     sum_h[2].pair()
-    deltas_of(3)
     out_sums(1)
-    hid[2].near()
-    hid[2].far()
-    sum_out.steps(0)
-    sum_h[1].pair()
-    deltas_of(2)
-    out_sums(2)
     hid[3].near()
     hid[3].far()
+    deltas_of(1)
+    sum_h[3].pair()
+    out_sums(3)
+    hid[0].near()
+    hidden_grad(0)
+    sum_out.step(3)
+    sum_out.step(2)
+    hid[2].far()
+    out_sums(2)
+    delta[1].near()
+    hid[0].far()
+    sum_out.step(7)
+    deltas_of(3)
+    sum_out.step(6)
+    out_sums(0)
+    delta[1].far()
     sum_h[0].pair()
-    sum_out.steps(1)
-    out_sums(3)
+    sum_out.step(5)
+    ing_sums(1)
+    deltas_of(2)
+    sum_out.step(1)
     delta[3].near()
-    deltas_of(1)
-    sum_out.steps(2)
+    sum_out.step(4)
+    delta[3].far()
+    ing_sums(3)
+    deltas_of(0)
+    sum_out.step(0)
     delta[2].near()
-    deltas_of(0)
-    sum_out.steps(3)
-    delta[3].far()
-    delta[1].near()
-    ing_sums(3)
+    sum_ing.step(3)
+    sum_ing.step(2)
     delta[2].far()
+    sum_ing.step(7)
+    ing_sums(2)
     delta[0].near()
-    ing_sums(2)
-    sum_ing.steps(3)
-    delta[1].far()
-    delta[0].far()
-    ing_sums(1)
-    ing_sums(0)
-    sum_ing.steps(2)
+    sum_ing.step(6)
     tiles(H // T, down_grad_tile)
     results[4].start()
-    sum_ing.steps(1)
+    delta[0].far()
+    sum_ing.step(5)
+    ing_sums(0)
+    sum_ing.step(4)
+    sum_out.finish()
+    results[0].start()
+    tiles(H // T, up_grad_tile)
+    results[3].start()
+    sum_ing.step(1)
     tiles(H // T, gate_grad_tile)
     results[2].start()
-    sum_ing.steps(0)
-    tiles(H // T, up_grad_tile)
-    results[3].start()
-    sum_out.finish()
-    results[0].start()
+    sum_ing.step(0)
     sum_ing.finish()
     results[1].start()
     for copy in pending[-POOL:]:
@@ -480,8 +500,10 @@
 
 def deliver(*refs):
     sources, results, held, sems = refs[:5], refs[5:10], refs[10:15], refs[15]
-    loads = [pltpu.make_async_copy(sources[i], held[i], sems.at[0, i]) for i in range(5)]
-    stores = [pltpu.make_async_copy(held[i], results[i], sems.at[1, i]) for i in range(5)]
+    pieces = [(i, pl.ds(row, 128)) for i in range(2, 5) for row in range(0, sources[i].shape[0], 128)]
+    pieces += [(i, pl.ds(0, B)) for i in range(2)]
+    loads = [pltpu.make_async_copy(sources[i].at[r], held[i].at[r], sems.at[0, n]) for n, (i, r) in enumerate(pieces)]
+    stores = [pltpu.make_async_copy(held[i].at[r], results[i].at[r], sems.at[1, n]) for n, (i, r) in enumerate(pieces)]
     for load in loads:
         load.start()
     for load, store in zip(loads, stores):
@@ -524,7 +546,7 @@
         out_shape=shapes,
         in_specs=[pl.BlockSpec(memory_space=pl.ANY)] * 5,
         out_specs=(pl.BlockSpec(memory_space=pl.ANY),) * 5,
-        scratch_shapes=[*[pltpu.VMEM(shape.shape, BF16) for shape in shapes], dma((2, 5))],
+        scratch_shapes=[*[pltpu.VMEM(shape.shape, BF16) for shape in shapes], dma((2, 16))],
         name="deliver",
     )(*results)
 

time: 90 us -> 86.8 us (0.964)
  Pallas kernels: 89.2 us -> 86 us
    pallas_call x1, Pallas kernels: 86.5 us -> 83.3 us  [body(): pl.pallas_call(kernel, out_shape=shapes, in_specs=[pl.BlockSpec(memory_sp...]
where the time goes in v4:
time: 86.8 us; the launch traced here: 86.7 us
  Pallas kernels  86 us (99%)
    pallas_call x1, Pallas kernels, body(): pl.pallas_call(kernel, out_shape=shapes, in_specs=[pl.BlockSpec(memory_sp...  83.3 us
    pallas_call x1, Pallas kernels, body(): pl.pallas_call(deliver, out_shape=shapes, in_specs=[pl.BlockSpec(memory_s...  2.73 us

profile of v4, /device:TPU:1, one launch (start us, length us, event | category | flops | bytes accessed | tf_op | source)
XLA Modules:
  0.0 86.7 jit_solution(9920222912966482719)
XLA Ops:
  0.6 83.3 %ffn.1 = (bf16[64,512]{1,0:T(8,128)(2,1)}, bf16[64,512]{1,0:T(8,128)(2,1)}, bf16[512,768]{1,0:T(8,128)(2,1)}, bf16[512,768]{1,0:T(8,128)(2,1)}, bf16[768,512]{1,0:T(8,128)(2,1)}) custom-call(bf16[64,512]{1,0:T(8,128)(2,1)} %x_hbm.1, bf16[512,768]{1,0:T(8,128)(2,1)} %wg_hbm.1, bf16[512,768]{1,0:T(8,128)(2,1)} %wu_hbm.1, bf16[768,512]{1,0:T(8,128)(2,1)} %wd_hbm.1, ...), custom_call_target="tpu_custom_call" | custom-call | tf_op jit(solution)/shard_map/ffn/pallas_call | solution.py:521
  83.9 2.7 %deliver.1 = (bf16[64,512]{1,0:T(8,128)(2,1)}, bf16[64,512]{1,0:T(8,128)(2,1)}, bf16[512,768]{1,0:T(8,128)(2,1)}, bf16[512,768]{1,0:T(8,128)(2,1)}, bf16[768,512]{1,0:T(8,128)(2,1)}) custom-call(bf16[64,512]{1,0:T(8,128)(2,1)} %get-tuple-element.10.refs_0_, bf16[64,512]{1,0:T(8,128)(2,1)} %get-tuple-element.11.refs_1_, ...), custom_call_target="tpu_custom_call" | custom-call | tf_op jit(solution)/shard_map/deliver/pallas_call | solution.py:544

commit v5 on v4

--- a/solution.py
+++ b/solution.py
@@ -401,8 +401,8 @@
     for i, (src, dst) in enumerate(((wg, wgs), (wu, wus), (wd, wds))):
         local[2 + i].wait()
         push(src, dst, wrecv.at[i], sibling)
+    gat_g.send_own()
     gat_x.pair()
-    gat_g.send_own()
     gat_x.step(1)
     gat_g.pair()
     for i, dst in enumerate((wgs, wus, wds)):
@@ -436,8 +436,8 @@
     hid[1].far()
     hidden_of(0)
     sum_h[1].pair()
+    sum_h[2].pair()
     hid[2].near()
-    sum_h[2].pair()
     out_sums(1)
     hid[3].near()
     hid[3].far()
@@ -484,9 +484,9 @@
     sum_ing.step(4)
     sum_out.finish()
     results[0].start()
+    sum_ing.step(1)
     tiles(H // T, up_grad_tile)
     results[3].start()
-    sum_ing.step(1)
     tiles(H // T, gate_grad_tile)
     results[2].start()
     sum_ing.step(0)

time: 86.8 us -> 85.9 us (0.990)
  Pallas kernels: 86 us -> 85.1 us
    pallas_call x1, Pallas kernels: 83.3 us -> 82.3 us  [body(): pl.pallas_call(kernel, out_shape=shapes, in_specs=[pl.BlockSpec(memory_sp...]
where the time goes in v5:
time: 85.9 us; the launch traced here: 85.7 us
  Pallas kernels  85.1 us (99%)
    pallas_call x1, Pallas kernels, body(): pl.pallas_call(kernel, out_shape=shapes, in_specs=[pl.BlockSpec(memory_sp...  82.3 us
    pallas_call x1, Pallas kernels, body(): pl.pallas_call(deliver, out_shape=shapes, in_specs=[pl.BlockSpec(memory_s...  2.73 us

profile of v5, /device:TPU:1, one launch (start us, length us, event | category | flops | bytes accessed | tf_op | source)
XLA Modules:
  0.0 85.7 jit_solution(7896954522979110673)
XLA Ops:
  0.6 82.3 %ffn.1 = (bf16[64,512]{1,0:T(8,128)(2,1)}, bf16[64,512]{1,0:T(8,128)(2,1)}, bf16[512,768]{1,0:T(8,128)(2,1)}, bf16[512,768]{1,0:T(8,128)(2,1)}, bf16[768,512]{1,0:T(8,128)(2,1)}) custom-call(bf16[64,512]{1,0:T(8,128)(2,1)} %x_hbm.1, bf16[512,768]{1,0:T(8,128)(2,1)} %wg_hbm.1, bf16[512,768]{1,0:T(8,128)(2,1)} %wu_hbm.1, bf16[768,512]{1,0:T(8,128)(2,1)} %wd_hbm.1, ...), custom_call_target="tpu_custom_call" | custom-call | tf_op jit(solution)/shard_map/ffn/pallas_call | solution.py:521
  83.0 2.7 %deliver.1 = (bf16[64,512]{1,0:T(8,128)(2,1)}, bf16[64,512]{1,0:T(8,128)(2,1)}, bf16[512,768]{1,0:T(8,128)(2,1)}, bf16[512,768]{1,0:T(8,128)(2,1)}, bf16[768,512]{1,0:T(8,128)(2,1)}) custom-call(bf16[64,512]{1,0:T(8,128)(2,1)} %get-tuple-element.10.refs_0_, bf16[64,512]{1,0:T(8,128)(2,1)} %get-tuple-element.11.refs_1_, ...), custom_call_target="tpu_custom_call" | custom-call | tf_op jit(solution)/shard_map/deliver/pallas_call | solution.py:544

commit v6 on v5

--- a/solution.py
+++ b/solution.py
@@ -18,7 +18,7 @@
 S = 8 // N
 C = S * B
 R = C // 8
-POOL = 48
+POOL = 24
 HID_STRAIGHT = (False, False, False, True)
 DELTA_STRAIGHT = (True, False, True, True)
 
@@ -68,7 +68,7 @@
         xall, gall, xsib, gsib, wg, wu, wd, wgs, wus, wds, pg, ph, pgf, phf,
         glanded, gtotal, ghalf, gother, hlanded, htotal, hhalf, hother, gu, hall, dall,
         po, pof, ro, so, zo, pi, pif, ri, si, zi, own, outv, ingv, ggv, ugv, dgv,
-        lsem, pool, wrecv, xr, xpr, gr, gpr, xsr, gsr, rgr, rhr, hr, dr, hsr, dsr, yr, zr, rsem,
+        lsem, pool, wrecv, xr, xpr, gr, gpr, xsr, gsr, rgr, rhr, hr, dr, hsr, dsr, yr, zr,
     ) = refs[5:]
     r = lax.axis_index("row")
     c = lax.axis_index("col")
@@ -390,7 +390,7 @@
         dgv[pl.ds(col, T), :] = tn(tokens(hall, col), gall[...].reshape(16 * B, F)).astype(BF16)
 
     results = [
-        pltpu.make_async_copy(src, dst, rsem.at[i]) for i, (src, dst) in enumerate(zip((outv, ingv, ggv, ugv, dgv), outs))
+        pltpu.make_async_copy(src, dst, lsem.at[i]) for i, (src, dst) in enumerate(zip((outv, ingv, ggv, ugv, dgv), outs))
     ]
 
     local[0].wait()
@@ -536,7 +536,7 @@
             dma((5,)), dma((POOL,)), dma((3,)),
             dma((2, 2, 4)), dma, dma((2, 2, 4)), dma, dma((N,)), dma((N,)),
             dma((N, 2)), dma((N, 2)), dma((N, 2, 1, 2)), dma((N, 2, 1, 2)), dma((N,)), dma((N,)),
-            dma((2, 8)), dma((2,)), dma((5,)),
+            dma((2, 8)), dma((2,)),
         ],
         compiler_params=pltpu.CompilerParams(collective_id=0, has_side_effects=True, vmem_limit_bytes=60 << 20),
         name="ffn",

time: 85.9 us -> 85.5 us (level)
  no operation moved by 1% of the time
where the time goes in v6:
time: 85.5 us; the launch traced here: 85.2 us
  Pallas kernels  84.5 us (99%)
    pallas_call x1, Pallas kernels, body(): pl.pallas_call(kernel, out_shape=shapes, in_specs=[pl.BlockSpec(memory_sp...  81.8 us
    pallas_call x1, Pallas kernels, body(): pl.pallas_call(deliver, out_shape=shapes, in_specs=[pl.BlockSpec(memory_s...  2.73 us

profile of v6, /device:TPU:1, one launch (start us, length us, event | category | flops | bytes accessed | tf_op | source)
XLA Modules:
  0.0 85.2 jit_solution(5375769975027978911)
XLA Ops:
  0.6 81.8 %ffn.1 = (bf16[64,512]{1,0:T(8,128)(2,1)}, bf16[64,512]{1,0:T(8,128)(2,1)}, bf16[512,768]{1,0:T(8,128)(2,1)}, bf16[512,768]{1,0:T(8,128)(2,1)}, bf16[768,512]{1,0:T(8,128)(2,1)}) custom-call(bf16[64,512]{1,0:T(8,128)(2,1)} %x_hbm.1, bf16[512,768]{1,0:T(8,128)(2,1)} %wg_hbm.1, bf16[512,768]{1,0:T(8,128)(2,1)} %wu_hbm.1, bf16[768,512]{1,0:T(8,128)(2,1)} %wd_hbm.1, ...), custom_call_target="tpu_custom_call" | custom-call | tf_op jit(solution)/shard_map/ffn/pallas_call | solution.py:521
  82.4 2.7 %deliver.1 = (bf16[64,512]{1,0:T(8,128)(2,1)}, bf16[64,512]{1,0:T(8,128)(2,1)}, bf16[512,768]{1,0:T(8,128)(2,1)}, bf16[512,768]{1,0:T(8,128)(2,1)}, bf16[768,512]{1,0:T(8,128)(2,1)}) custom-call(bf16[64,512]{1,0:T(8,128)(2,1)} %get-tuple-element.10.refs_0_, bf16[64,512]{1,0:T(8,128)(2,1)} %get-tuple-element.11.refs_1_, ...), custom_call_target="tpu_custom_call" | custom-call | tf_op jit(solution)/shard_map/deliver/pallas_call | solution.py:544

commit v7 on v6

--- a/solution.py
+++ b/solution.py
@@ -433,10 +433,10 @@
     hidden_of(2)
     hidden_of(3)
     hidden_grad(3)
+    sum_h[2].pair()
     hid[1].far()
     hidden_of(0)
     sum_h[1].pair()
-    sum_h[2].pair()
     hid[2].near()
     out_sums(1)
     hid[3].near()
@@ -484,9 +484,9 @@
     sum_ing.step(4)
     sum_out.finish()
     results[0].start()
-    sum_ing.step(1)
     tiles(H // T, up_grad_tile)
     results[3].start()
+    sum_ing.step(1)
     tiles(H // T, gate_grad_tile)
     results[2].start()
     sum_ing.step(0)

time: 85.5 us -> 86.6 us (1.013)
  Pallas kernels: 84.5 us -> 85.8 us
    pallas_call x1, Pallas kernels: 81.8 us -> 83.1 us  [body(): pl.pallas_call(kernel, out_shape=shapes, in_specs=[pl.BlockSpec(memory_sp...]
where the time goes in v7:
time: 86.6 us; the launch traced here: 86.4 us
  Pallas kernels  85.8 us (99%)
    pallas_call x1, Pallas kernels, body(): pl.pallas_call(kernel, out_shape=shapes, in_specs=[pl.BlockSpec(memory_sp...  83.1 us
    pallas_call x1, Pallas kernels, body(): pl.pallas_call(deliver, out_shape=shapes, in_specs=[pl.BlockSpec(memory_s...  2.73 us

profile of v7, /device:TPU:1, one launch (start us, length us, event | category | flops | bytes accessed | tf_op | source)
XLA Modules:
  0.0 86.4 jit_solution(12427663601021851274)
XLA Ops:
  0.6 83.1 %ffn.1 = (bf16[64,512]{1,0:T(8,128)(2,1)}, bf16[64,512]{1,0:T(8,128)(2,1)}, bf16[512,768]{1,0:T(8,128)(2,1)}, bf16[512,768]{1,0:T(8,128)(2,1)}, bf16[768,512]{1,0:T(8,128)(2,1)}) custom-call(bf16[64,512]{1,0:T(8,128)(2,1)} %x_hbm.1, bf16[512,768]{1,0:T(8,128)(2,1)} %wg_hbm.1, bf16[512,768]{1,0:T(8,128)(2,1)} %wu_hbm.1, bf16[768,512]{1,0:T(8,128)(2,1)} %wd_hbm.1, ...), custom_call_target="tpu_custom_call" | custom-call | tf_op jit(solution)/shard_map/ffn/pallas_call | solution.py:521
  83.7 2.7 %deliver.1 = (bf16[64,512]{1,0:T(8,128)(2,1)}, bf16[64,512]{1,0:T(8,128)(2,1)}, bf16[512,768]{1,0:T(8,128)(2,1)}, bf16[512,768]{1,0:T(8,128)(2,1)}, bf16[768,512]{1,0:T(8,128)(2,1)}) custom-call(bf16[64,512]{1,0:T(8,128)(2,1)} %get-tuple-element.10.refs_0_, bf16[64,512]{1,0:T(8,128)(2,1)} %get-tuple-element.11.refs_1_, ...), custom_call_target="tpu_custom_call" | custom-call | tf_op jit(solution)/shard_map/deliver/pallas_call | solution.py:544
